TPU v7x, 128 devices: a whole 4x4x4 slice. The times are simulated.
128 devices in a mesh: ctx: 32 (over z, y, core), ch: 4 (over x).
Axes of the slice: x: 4, y: 4, z: 4, core: 2. Of those that a mesh axis runs over, the one named last changes fastest.
Arguments:
- q_in: bfloat16 [16384, 4096], P('ctx', 'ch'), may hold values from -6 to 6
- k_in: bfloat16 [16384, 4096], P('ctx', 'ch'), may hold values from -6 to 6
- v_in: bfloat16 [16384, 4096], P('ctx', 'ch'), may hold values from -6 to 6
- out_grad: bfloat16 [16384, 4096], P('ctx', 'ch'), may hold values from -6 to 6
- filters: float32 [16384, 1024], P('ctx'), may hold values from -1.5 to 1.5
- skip: float32 [4096], P('ch'), may hold values from 0.5 to 2
Outputs:
- q_grad: bfloat16 [16384, 4096], P('ctx', 'ch')
- k_grad: bfloat16 [16384, 4096], P('ctx', 'ch')
- v_grad: bfloat16 [16384, 4096], P('ctx', 'ch')
- filter_grad: float32 [16384, 1024], P('ctx', 'ch')
All inputs are finite; a program needn't handle non-finite values.
Results may differ from a plain program's by a relative error of at most 0.007.
Values may be sent and summed in bfloat16 or wider, within the bound.
No kernel may reach another device: no remote copies, remote signals or barrier semaphores. Data moves between devices by JAX's collectives and lax.ppermute only.
A program may use at most 192 MiB of HBM per device.

v0:
```python
import math

import jax
import jax.numpy as jnp
from jax import lax
from jax.sharding import PartitionSpec as P

HIGH = lax.Precision.HIGHEST


def phase_table(left_index, right_index, period):
    product = left_index[:, None] * right_index[None, :] % period
    angle = product.astype(jnp.float32) * (2.0 * math.pi / period)
    return (jnp.cos(angle), jnp.sin(angle))


def multiply(form, table, data, low):
    if low:
        return jnp.einsum(
            form, table.astype(jnp.bfloat16), data, preferred_element_type=jnp.float32
        )
    return jnp.einsum(form, table, data, precision=HIGH)


def forward_blocks(segments, block_count, period):
    span = segments[0].shape[1]
    frequency = jnp.arange(2 * block_count, dtype=jnp.int32)
    cos_block, sin_block = phase_table(
        frequency, jnp.arange(block_count, dtype=jnp.int32), 2 * block_count
    )
    cos_twist, sin_twist = phase_table(frequency, jnp.arange(span, dtype=jnp.int32), period)
    results = []
    for segment in segments:
        real_part = multiply("ka,ajc->kjc", cos_block, segment, True)
        imag_part = -multiply("ka,ajc->kjc", sin_block, segment, True)
        results.append(
            (real_part * cos_twist[:, :, None] + imag_part * sin_twist[:, :, None]).astype(
                jnp.bfloat16
            )
        )
        results.append(
            (imag_part * cos_twist[:, :, None] - real_part * sin_twist[:, :, None]).astype(
                jnp.bfloat16
            )
        )
    return results


def row_transform(parts, inverse_sign, low):
    length = parts[0].shape[1]
    index_row = jnp.arange(length, dtype=jnp.int32)
    cos_row, sin_row = phase_table(index_row, index_row, length)
    results = []
    for position in range(0, len(parts), 2):
        real_part = parts[position]
        imag_part = parts[position + 1]
        cos_real = multiply("qj,kjc->kqc", cos_row, real_part, low)
        cos_imag = multiply("qj,kjc->kqc", cos_row, imag_part, low)
        sin_real = multiply("qj,kjc->kqc", sin_row, real_part, low)
        sin_imag = multiply("qj,kjc->kqc", sin_row, imag_part, low)
        if inverse_sign:
            results.append(cos_real - sin_imag)
            results.append(cos_imag + sin_real)
        else:
            results.append(cos_real + sin_imag)
            results.append(cos_imag - sin_real)
    return results


def inverse_blocks(parts, block_count, period, low):
    span = parts[0].shape[1]
    frequency = jnp.arange(2 * block_count, dtype=jnp.int32)
    cos_twist, sin_twist = phase_table(frequency, jnp.arange(span, dtype=jnp.int32), period)
    cos_block, sin_block = phase_table(
        jnp.arange(block_count, dtype=jnp.int32), frequency, 2 * block_count
    )
    results = []
    for position in range(0, len(parts), 2):
        real_part = (
            parts[position] * cos_twist[:, :, None] - parts[position + 1] * sin_twist[:, :, None]
        )
        imag_part = (
            parts[position + 1] * cos_twist[:, :, None] + parts[position] * sin_twist[:, :, None]
        )
        if low:
            real_part = real_part.astype(jnp.bfloat16)
            imag_part = imag_part.astype(jnp.bfloat16)
        summed = multiply("ak,kjc->ajc", cos_block, real_part, low) - multiply(
            "ak,kjc->ajc", sin_block, imag_part, low
        )
        results.append(summed * (1.0 / period))
    return results


def body(q_in, k_in, v_in, out_grad, filters, skip):
    ctx_count = lax.axis_size("ctx")
    ch_count = lax.axis_size("ch")
    seq_rows, local_width = q_in.shape
    period = 2 * seq_rows * ctx_count
    narrow = local_width // (ctx_count * ch_count)
    gated_low = (k_in.astype(jnp.float32) * v_in.astype(jnp.float32)).astype(jnp.bfloat16)
    grad_low = (q_in.astype(jnp.float32) * out_grad.astype(jnp.float32)).astype(jnp.bfloat16)
    filters_low = filters.astype(jnp.bfloat16)
    gated = lax.optimization_barrier(gated_low).astype(jnp.float32)
    grad_gated = lax.optimization_barrier(grad_low).astype(jnp.float32)

    def regroup(field):
        return (
            field.reshape(seq_rows, ch_count, ctx_count, narrow)
            .transpose(0, 2, 1, 3)
            .reshape(1, seq_rows, local_width)
        )

    def ungroup(field):
        return (
            field.reshape(seq_rows, ctx_count, ch_count, narrow)
            .transpose(0, 2, 1, 3)
            .reshape(seq_rows, local_width)
        )

    gated_cols, grad_cols, filter_cols = (
        lax.all_to_all(regroup(gated_low), "ctx", split_axis=2, concat_axis=0, tiled=True),
        lax.all_to_all(regroup(grad_low), "ctx", split_axis=2, concat_axis=0, tiled=True),
        lax.all_to_all(regroup(filters_low), "ctx", split_axis=2, concat_axis=0, tiled=True),
    )
    spectra = row_transform(
        forward_blocks([gated_cols, grad_cols, filter_cols], ctx_count, period), False, True
    )
    gated_re, gated_im, grad_re, grad_im, filt_re, filt_im = spectra
    state_re = (gated_re * filt_re - gated_im * filt_im).astype(jnp.bfloat16)
    state_im = (gated_re * filt_im + gated_im * filt_re).astype(jnp.bfloat16)
    back_re = (grad_re * filt_re + grad_im * filt_im).astype(jnp.bfloat16)
    back_im = (grad_im * filt_re - grad_re * filt_im).astype(jnp.bfloat16)
    taps_re = grad_re * gated_re + grad_im * gated_im
    taps_im = grad_im * gated_re - grad_re * gated_im
    low_rows = row_transform([state_re, state_im, back_re, back_im], True, True)
    taps_rows = row_transform([taps_re, taps_im], True, False)
    state_blk, back_blk = inverse_blocks(low_rows, ctx_count, period, True)
    taps_blk = inverse_blocks(taps_rows, ctx_count, period, False)[0]
    state_seq, back_seq, taps_seq = (
        lax.all_to_all(state_blk, "ctx", split_axis=0, concat_axis=2, tiled=True),
        lax.all_to_all(back_blk, "ctx", split_axis=0, concat_axis=2, tiled=True),
        lax.all_to_all(taps_blk, "ctx", split_axis=0, concat_axis=2, tiled=True),
    )
    conv_state = ungroup(state_seq)
    conv_back = ungroup(back_seq)
    taps_local = ungroup(taps_seq)
    taps_total = lax.psum_scatter(taps_local, "ch", scatter_dimension=1, tiled=True)
    mixed_state = conv_state + skip[None, :] * gated
    gated_back = conv_back + skip[None, :] * grad_gated
    q_grad = (out_grad.astype(jnp.float32) * mixed_state).astype(jnp.bfloat16)
    k_grad = (gated_back * v_in.astype(jnp.float32)).astype(jnp.bfloat16)
    v_grad = (gated_back * k_in.astype(jnp.float32)).astype(jnp.bfloat16)
    scale_factor = 1.0 / math.sqrt(seq_rows * ctx_count * ch_count)
    filter_grad = taps_total * scale_factor
    return (q_grad, k_grad, v_grad, filter_grad)


def solution(mesh):
    return jax.shard_map(
        body,
        mesh=mesh,
        in_specs=(
            P("ctx", "ch"),
            P("ctx", "ch"),
            P("ctx", "ch"),
            P("ctx", "ch"),
            P("ctx", None),
            P("ch"),
        ),
        out_specs=(P("ctx", "ch"), P("ctx", "ch"), P("ctx", "ch"), P("ctx", "ch")),
        check_vma=False,
    )
```

profile of v0, /device:TPU:1, one launch (start us, length us, event | category | flops | bytes accessed | tf_op | source)
XLA Modules:
  0.0 463.1 jit_solution(159604348048424883)
XLA Ops:
  15.5 8.0 %reduce.2 = bf16[1024,512]{1,0:T(8,128)(2,1)S(1)} reduce(bf16[1024,1,512]{2,1,0:T(2,128)(2,1)} %bitcast.222, bf16[]{:T(256)} %broadcast.362), dimensions={1}, to_apply=%bitcast.209.reduce_sub_computation | reduce | bytes 2097154
  25.1 9.9 %all-to-all-start = ((bf16[32,2,8192]{2,1,0:T(2,128)(2,1)}), bf16[32,2,8192]{2,1,0:T(2,128)(2,1)S(1)}, u32[]{:S(2)}, u32[]{:S(2)}) async-start(bf16[32,2,8192]{2,1,0:T(2,128)(2,1)} %reshape.106), calls=%async_computation | async-start | bytes 2097152 | tf_op jit(solution)/shard_map/all_to_all | solution.py:122
  38.6 8.0 %reduce.1 = bf16[1024,512]{1,0:T(8,128)(2,1)} reduce(bf16[1024,1,512]{2,1,0:T(2,128)(2,1)S(1)} %bitcast.224, bf16[]{:T(256)} %broadcast.362), dimensions={1}, to_apply=%bitcast.208.reduce_sub_computation | reduce | bytes 2097154
  76.6 7.9 %all-to-all-start.3 = ((bf16[32,2,8192]{2,1,0:T(2,128)(2,1)}), bf16[32,2,8192]{2,1,0:T(2,128)(2,1)}, u32[]{:S(2)}, u32[]{:S(2)}) async-start(bf16[32,2,8192]{2,1,0:T(2,128)(2,1)} %reshape.110), calls=%async_computation.3 | async-start | bytes 2097152 | tf_op jit(solution)/shard_map/all_to_all | solution.py:123
  109.4 8.4 %add_convert_fusion.2 = (bf16[64,512,32]{1,0,2:T(8,128)(2,1)}, bf16[64,512,32]{1,0,2:T(8,128)(2,1)}, bf16[64,512,32]{1,0,2:T(8,128)(2,1)}, bf16[64,512,32]{1,0,2...) fusion(f32[64,512,32]{1,0,2:T(8,128)S(1)} %fusion.70, ...), kind=kOutput, calls=%fused_computation.21 | convolution fusion | flops 95451136 | bytes 34865152 | tf_op jit(solution)/shard_map/ka,ajc->kjc/dot_general | solution.py:19
  117.8 8.0 %fusion.43 = f32[64,32,512]{2,1,0:T(8,128)S(1)} fusion(bf16[64,512,32]{1,0,2:T(8,128)(2,1)} %get-tuple-element.26), kind=kOutput, calls=%fused_computation.77 | convolution fusion | flops 1077673984 | bytes 6291456 | tf_op jit(solution)/shard_map/qj,kjc->kqc/dot_general | solution.py:19
  154.5 8.2 %convolution_subtract_fusion.3 = f32[64,32,512]{2,1,0:T(8,128)} fusion(f32[64,32,512]{2,1,0:T(8,128)S(1)} %fusion.45, bf16[64,512,32]{1,0,2:T(8,128)(2,1)S(1)} %copy-done.21), kind=kOutput, calls=%fused_computation.41 | convolution fusion | flops 1078722560 | bytes 10485760 | tf_op jit(solution)/shard_map/qj,kjc->kqc/dot_general | solution.py:19
  162.7 8.2 %convolution_add_fusion.3 = f32[64,32,512]{2,1,0:T(8,128)} fusion(f32[64,32,512]{2,1,0:T(8,128)S(1)} %fusion.49, bf16[64,512,32]{1,0,2:T(8,128)(2,1)S(1)} %copy-done.20), kind=kOutput, calls=%fused_computation.43 | convolution fusion | flops 1078722560 | bytes 10485760 | tf_op jit(solution)/shard_map/qj,kjc->kqc/dot_general | solution.py:19
  176.5 8.3 %fusion.55 = f32[64,32,512]{2,1,0:T(8,128)} fusion(bf16[64,512,32]{1,0,2:T(8,128)(2,1)S(1)} %get-tuple-element.47), kind=kOutput, calls=%fused_computation.89 | convolution fusion | flops 1077673984 | bytes 6291456 | tf_op jit(solution)/shard_map/qj,kjc->kqc/dot_general | solution.py:19
  184.8 8.1 %convolution_subtract_fusion.4 = f32[64,32,512]{2,1,0:T(8,128)} fusion(f32[64,32,512]{2,1,0:T(8,128)S(1)} %fusion.51, bf16[64,512,32]{1,0,2:T(8,128)(2,1)S(1)} %get-tuple-element.47), kind=kOutput, calls=%fused_computation.42 | convolution fusion | flops 1078722560 | bytes 10485760 | tf_op jit(solution)/shard_map/qj,kjc->kqc/dot_general | solution.py:19
  193.0 14.0 %multiply_add_fusion = (f32[64,32,512]{2,1,0:T(8,128)S(1)}, f32[64,32,512]{2,1,0:T(8,128)S(1)}, bf16[64,512,32]{1,2,0:T(8,128)(2,1)S(1)}, bf16[64,512,32]{1,2,0:...) fusion(f32[64,32,512]{2,1,0:T(8,128)S(1)} %convolution_subtract_fusion.1, ...), kind=kOutput, calls=%fused_computation.15 | convolution fusion | flops 1101791232 | bytes 44040192 | tf_op jit(solution)/shard_map/qj,kjc->kqc/dot_general | solution.py:19
  207.0 12.3 %fusion = f32[64,32,512]{2,1,0:T(8,128)} fusion(f32[64,32,512]{2,1,0:T(8,128)S(1)} %get-tuple-element.17), kind=kOutput, calls=%fused_computation | convolution fusion | flops 6446120960 | bytes 8388608 | tf_op jit(solution)/shard_map/qj,kjc->kqc/dot_general | solution.py:22
  219.3 10.7 %fusion.2 = f32[64,32,512]{2,1,0:T(8,128)S(1)} fusion(f32[64,32,512]{2,1,0:T(8,128)S(1)} %get-tuple-element.17), kind=kOutput, calls=%fused_computation.2 | convolution fusion | flops 6446120960 | bytes 8388608 | tf_op jit(solution)/shard_map/qj,kjc->kqc/dot_general | solution.py:22
  230.0 7.5 %fusion.109 = f32[64,32,512]{2,1,0:T(8,128)S(1)} fusion(bf16[64,512,32]{1,2,0:T(8,128)(2,1)S(1)} %get-tuple-element.34), kind=kOutput, calls=%fused_computation.140 | convolution fusion | flops 1077673984 | bytes 6291456 | tf_op jit(solution)/shard_map/qj,kjc->kqc/dot_general | solution.py:19
  244.7 7.6 %convolution_subtract_fusion.2 = f32[64,32,512]{2,1,0:T(8,128)} fusion(f32[64,32,512]{2,1,0:T(8,128)S(1)} %fusion.109, bf16[64,512,32]{1,2,0:T(8,128)(2,1)S(1)} %get-tuple-element.35), kind=kOutput, calls=%fused_computation.40 | convolution fusion | flops 1078722560 | bytes 10485760 | tf_op jit(solution)/shard_map/qj,kjc->kqc/dot_general | solution.py:19
  252.3 7.7 %convolution_add_fusion.2 = f32[64,32,512]{2,1,0:T(8,128)} fusion(f32[64,32,512]{2,1,0:T(8,128)S(1)} %fusion.107, bf16[64,512,32]{1,2,0:T(8,128)(2,1)S(1)} %get-tuple-element.34), kind=kOutput, calls=%fused_computation.39 | convolution fusion | flops 1078722560 | bytes 10485760 | tf_op jit(solution)/shard_map/qj,kjc->kqc/dot_general | solution.py:19
  267.3 7.7 %fusion.101 = f32[64,32,512]{2,1,0:T(8,128)S(1)} fusion(bf16[64,512,32]{1,2,0:T(8,128)(2,1)S(1)} %get-tuple-element.37), kind=kOutput, calls=%fused_computation.132 | convolution fusion | flops 1077673984 | bytes 6291456 | tf_op jit(solution)/shard_map/qj,kjc->kqc/dot_general | solution.py:19
  274.9 7.7 %convolution_subtract_fusion = f32[64,32,512]{2,1,0:T(8,128)} fusion(f32[64,32,512]{2,1,0:T(8,128)S(1)} %fusion.103, bf16[64,512,32]{1,2,0:T(8,128)(2,1)S(1)} %get-tuple-element.37), kind=kOutput, calls=%fused_computation.36 | convolution fusion | flops 1078722560 | bytes 10485760 | tf_op jit(solution)/shard_map/qj,kjc->kqc/dot_general | solution.py:19
  282.6 7.6 %convolution_add_fusion = f32[64,32,512]{2,1,0:T(8,128)} fusion(f32[64,32,512]{2,1,0:T(8,128)S(1)} %fusion.101, bf16[64,512,32]{1,2,0:T(8,128)(2,1)S(1)} %get-tuple-element.36), kind=kOutput, calls=%fused_computation.35 | convolution fusion | flops 1078722560 | bytes 10485760 | tf_op jit(solution)/shard_map/qj,kjc->kqc/dot_general | solution.py:19
  290.2 12.2 %fusion.12 = f32[64,32,512]{2,1,0:T(8,128)} fusion(f32[64,32,512]{2,1,0:T(8,128)S(1)} %fusion.2, f32[64,32,512]{2,1,0:T(8,128)S(1)} %get-tuple-element.16), kind=kOutput, calls=%fused_computation.45 | convolution fusion | flops 6447169536 | bytes 12582912 | tf_op jit(solution)/shard_map/qj,kjc->kqc/dot_general | solution.py:22
  302.4 20.6 %subtract_bitcast_fusion = (f32[64,512,32]{1,2,0:T(8,128)}, f32[64,512,32]{1,2,0:T(8,128)}, bf16[64,512,32]{1,2,0:T(8,128)(2,1)}, bf16[64,512,32]{1,2,0:T(8,128)...) fusion(f32[64,32,512]{2,1,0:T(8,128)} %fusion.12, f32[64,512]{1,0:T(8,128)S(1)} %get-tuple-element.49, ...), kind=kOutput, calls=%fused_computation.13 | convolution fusion | flops 6470238208 | bytes 46399488 | tf_op jit(solution)/shard_map/qj,kjc->kqc/dot_general | solution.py:22
  354.6 18.1 %all-to-all-done.5 = f32[32,512,32]{1,2,0:T(8,128)} async-done(((f32[32,512,32]{1,2,0:T(8,128)}), f32[32,512,32]{1,2,0:T(8,128)}, u32[]{:S(2)}, u32[]{:S(2)}) %all-to-all-start.5) | async-done | bytes 2097184 | tf_op jit(solution)/shard_map/all_to_all | solution.py:143
  392.8 14.7 %all-to-all-done.4 = f32[32,512,32]{1,2,0:T(8,128)} async-done(((f32[32,512,32]{1,2,0:T(8,128)}), f32[32,512,32]{1,2,0:T(8,128)}, u32[]{:S(2)}, u32[]{:S(2)}) %all-to-all-start.4) | async-done | bytes 2097184 | tf_op jit(solution)/shard_map/all_to_all | solution.py:142
  417.6 24.6 %all-to-all-done.2 = f32[32,512,32]{1,2,0:T(8,128)} async-done(((f32[32,512,32]{1,2,0:T(8,128)}), f32[32,512,32]{1,2,0:T(8,128)}, u32[]{:S(2)}, u32[]{:S(2)}) %all-to-all-start.2) | async-done | bytes 2097184 | tf_op jit(solution)/shard_map/all_to_all | solution.py:141
  (118 shorter events, 192.0 us)
Async XLA Ops:
  8.7 6.3 %copy-start.3 = (bf16[512,1024]{0,1:T(8,128)(2,1)}, bf16[512,1024]{0,1:T(8,128)(2,1)S(1)}, u32[]{:S(2)}) copy-start(bf16[512,1024]{0,1:T(8,128)(2,1)S(1)} %copy.107) | copy-start | bytes 3145732
  25.1 27.0 %all-to-all-start = ((bf16[32,2,8192]{2,1,0:T(2,128)(2,1)}), bf16[32,2,8192]{2,1,0:T(2,128)(2,1)S(1)}, u32[]{:S(2)}, u32[]{:S(2)}) async-start(bf16[32,2,8192]{2,1,0:T(2,128)(2,1)} %reshape.106), calls=%async_computation | async-start | bytes 2097152 | tf_op jit(solution)/shard_map/all_to_all | solution.py:122
  46.6 10.8 %copy-start.24 = (bf16[512,1024]{1,0:T(8,128)(2,1)S(1)}, bf16[512,1024]{1,0:T(8,128)(2,1)}, u32[]{:S(2)}) copy-start(bf16[512,1024]{1,0:T(8,128)(2,1)} %param.9) | copy-start | bytes 3145732
  52.1 8.0 %copy-start.18 = (bf16[32,2,8192]{2,1,0:T(2,128)(2,1)}, bf16[32,2,8192]{2,1,0:T(2,128)(2,1)S(1)}, u32[]{:S(2)}) copy-start(bf16[32,2,8192]{2,1,0:T(2,128)(2,1)S(1)} %all-to-all-done) | copy-start | bytes 3145732
  52.1 24.5 %all-to-all-start.1 = ((bf16[32,2,8192]{2,1,0:T(2,128)(2,1)}), bf16[32,2,8192]{2,1,0:T(2,128)(2,1)}, u32[]{:S(2)}, u32[]{:S(2)}) async-start(bf16[32,2,8192]{2,1,0:T(2,128)(2,1)} %reshape.108), calls=%async_computation.1 | async-start | bytes 2097152 | tf_op jit(solution)/shard_map/all_to_all | solution.py:124
  57.9 4.9 %copy-start.9 = (bf16[512,1024]{0,1:T(8,128)(2,1)}, bf16[512,1024]{0,1:T(8,128)(2,1)S(1)}, u32[]{:S(2)}) copy-start(bf16[512,1024]{0,1:T(8,128)(2,1)S(1)} %copy.106) | copy-start | bytes 3145732
  76.6 25.0 %all-to-all-start.3 = ((bf16[32,2,8192]{2,1,0:T(2,128)(2,1)}), bf16[32,2,8192]{2,1,0:T(2,128)(2,1)}, u32[]{:S(2)}, u32[]{:S(2)}) async-start(bf16[32,2,8192]{2,1,0:T(2,128)(2,1)} %reshape.110), calls=%async_computation.3 | async-start | bytes 2097152 | tf_op jit(solution)/shard_map/all_to_all | solution.py:123
  117.8 53.2 %copy-start.16 = (bf16[64,512,32]{1,0,2:T(8,128)(2,1)}, bf16[64,512,32]{1,0,2:T(8,128)(2,1)S(1)}, u32[]{:S(2)}) copy-start(bf16[64,512,32]{1,0,2:T(8,128)(2,1)S(1)} %get-tuple-element.46) | copy-start | bytes 6291460
  117.8 8.0 %copy-start.23 = (bf16[64,512,32]{1,0,2:T(8,128)(2,1)S(1)}, bf16[64,512,32]{1,0,2:T(8,128)(2,1)}, u32[]{:S(2)}) copy-start(bf16[64,512,32]{1,0,2:T(8,128)(2,1)} %get-tuple-element.27) | copy-start | bytes 6291460
  131.3 6.2 %copy-start.22 = (bf16[64,512,32]{1,0,2:T(8,128)(2,1)S(1)}, bf16[64,512,32]{1,0,2:T(8,128)(2,1)}, u32[]{:S(2)}) copy-start(bf16[64,512,32]{1,0,2:T(8,128)(2,1)} %get-tuple-element.26) | copy-start | bytes 6291460
  137.5 5.8 %copy-start.20 = (bf16[64,512,32]{1,0,2:T(8,128)(2,1)S(1)}, bf16[64,512,32]{1,0,2:T(8,128)(2,1)}, u32[]{:S(2)}) copy-start(bf16[64,512,32]{1,0,2:T(8,128)(2,1)} %get-tuple-element.44) | copy-start | bytes 6291460
  143.3 5.7 %copy-start.21 = (bf16[64,512,32]{1,0,2:T(8,128)(2,1)S(1)}, bf16[64,512,32]{1,0,2:T(8,128)(2,1)}, u32[]{:S(2)}) copy-start(bf16[64,512,32]{1,0,2:T(8,128)(2,1)} %get-tuple-element.45) | copy-start | bytes 6291460
  184.8 8.1 %copy-start.17 = (bf16[64,512,32]{1,0,2:T(8,128)(2,1)S(1)}, bf16[64,512,32]{1,0,2:T(8,128)(2,1)}, u32[]{:S(2)}) copy-start(bf16[64,512,32]{1,0,2:T(8,128)(2,1)} %copy-done.16) | copy-start | bytes 6291460
  323.0 7.3 %copy-start.2 = (f32[64,512,32]{1,2,0:T(8,128)S(1)}, f32[64,512,32]{1,2,0:T(8,128)}, u32[]{:S(2)}) copy-start(f32[64,512,32]{1,2,0:T(8,128)} %get-tuple-element.22) | copy-start | bytes 12582916
  337.6 11.7 %copy-start.14 = (bf16[64,512,32]{1,2,0:T(8,128)(2,1)S(1)}, bf16[64,512,32]{1,2,0:T(8,128)(2,1)}, u32[]{:S(2)}) copy-start(bf16[64,512,32]{1,2,0:T(8,128)(2,1)} %get-tuple-element.41) | copy-start | bytes 6291460
  337.6 35.1 %all-to-all-start.5 = ((f32[32,512,32]{1,2,0:T(8,128)}), f32[32,512,32]{1,2,0:T(8,128)}, u32[]{:S(2)}, u32[]{:S(2)}) async-start(f32[32,512,32]{1,2,0:T(8,128)} %copy.142), calls=%async_computation.5 | async-start | bytes 4194304 | tf_op jit(solution)/shard_map/all_to_all | solution.py:143
  372.7 34.7 %all-to-all-start.4 = ((f32[32,512,32]{1,2,0:T(8,128)}), f32[32,512,32]{1,2,0:T(8,128)}, u32[]{:S(2)}, u32[]{:S(2)}) async-start(f32[32,512,32]{1,2,0:T(8,128)} %copy.138), calls=%async_computation.4 | async-start | bytes 4194304 | tf_op jit(solution)/shard_map/all_to_all | solution.py:142
  379.4 74.2 %reduce-scatter.2.cloned.1.call-start = ((), (), s32[]{:S(2)}) async-start(), calls=%async_computation.7 | async-start | bytes 2621440 | tf_op jit(solution)/shard_map/reduce_scatter | solution.py:148
  407.4 34.7 %all-to-all-start.2 = ((f32[32,512,32]{1,2,0:T(8,128)}), f32[32,512,32]{1,2,0:T(8,128)}, u32[]{:S(2)}, u32[]{:S(2)}) async-start(f32[32,512,32]{1,2,0:T(8,128)} %copy.126), calls=%async_computation.2 | async-start | bytes 4194304 | tf_op jit(solution)/shard_map/all_to_all | solution.py:141
  414.2 29.9 %copy-start.4 = (bf16[512,1024]{0,1:T(8,128)(2,1)S(1)}, bf16[512,1024]{0,1:T(8,128)(2,1)}, u32[]{:S(2)}) copy-start(bf16[512,1024]{0,1:T(8,128)(2,1)} %copy-done.3) | copy-start | bytes 3145732
  414.2 29.9 %copy-start.6 = (bf16[512,1024]{0,1:T(8,128)(2,1)S(1)}, bf16[512,1024]{0,1:T(8,128)(2,1)}, u32[]{:S(2)}) copy-start(bf16[512,1024]{0,1:T(8,128)(2,1)} %copy-done.5) | copy-start | bytes 3145732
  414.2 29.9 %copy-start.8 = (bf16[512,1024]{0,1:T(8,128)(2,1)S(1)}, bf16[512,1024]{0,1:T(8,128)(2,1)}, u32[]{:S(2)}) copy-start(bf16[512,1024]{0,1:T(8,128)(2,1)} %copy-done.7) | copy-start | bytes 3145732
  414.2 29.9 %copy-start.25 = (f32[1024]{0:T(1024)S(1)}, f32[1024]{0:T(1024)}, u32[]{:S(2)}) copy-start(f32[1024]{0:T(1024)} %param.11) | copy-start | bytes 12292
  447.7 4.6 copy-start.19
  (9 other events, 23.5 us)
Sparse Core Ops, SparseCore 0:
  383.1 30.7 reduce-scatter.1
where the time goes:
time: 472 us; the launch traced here: 463 us
  matrix products  252 us (53%)
  local copies, waits for them, and re-layouts  62.5 us (13%)
  waiting for transfers between devices  60.8 us (13%)
  starting transfers between devices  44.3 us (9%)
  other arithmetic  28 us (6%)
  between operations  15.1 us (3%)
    dot_general x30, matrix products, multiply(): jnp.einsum(form, table.astype(jnp.bfloat16), data, preferred_element_type...  185 us
    dot_general x6, matrix products, multiply(): return jnp.einsum(form, table, data, precision=HIGH)  67.7 us
    unnamed x71, local copies, waits for them, and re-layouts  39.7 us
    all_to_all x1, waiting for transfers between devices, body(): lax.all_to_all(state_blk, 'ctx', split_axis=0, concat_axis=2, tiled=True)  24.6 us
    unnamed x3, other arithmetic  23.1 us
    all_to_all x1, waiting for transfers between devices, body(): lax.all_to_all(taps_blk, 'ctx', split_axis=0, concat_axis=2, tiled=True)  18.1 us
    all_to_all x1, waiting for transfers between devices, body(): lax.all_to_all(back_blk, 'ctx', split_axis=0, concat_axis=2, tiled=True)  14.7 us
    all_to_all x1, starting transfers between devices, body(): lax.all_to_all(regroup(gated_low), 'ctx', split_axis=2, concat_axis=0, ti...  9.93 us
  transfers between devices with their start and end apart: 7, of which 5 were waited for; matrix products, arithmetic and copies ran while one was open for 18% of the time, Pallas kernels for 0%

commit v1 on v0

v1 whole, which is shorter than its diff:
```python
import functools
import math

import jax
import jax.numpy as jnp
import ml_dtypes
import numpy as np
from jax import lax
from jax.experimental import pallas as pl
from jax.experimental.pallas import tpu as pltpu
from jax.sharding import PartitionSpec as P

BF = jnp.bfloat16
F32 = jnp.float32

A = 32
X = 4
DEV = A * X
L = 128
SEG = 4 * L
KH = A + 1
PERIOD = 2 * A * SEG
ROWS = 72
MIB = 1024 * 1024


def low(table):
    return np.asarray(table, np.float32).astype(ml_dtypes.bfloat16)


def spread(table, count):
    return np.kron(table, np.eye(count))


@functools.cache
def constants():
    k = np.arange(KH)[:, None]
    a = np.arange(A)[None, :]
    angle = 2 * np.pi * (k * a % (2 * A)) / (2 * A)
    cos_block = low(np.cos(angle)).astype(np.float64)
    sin_block = low(np.sin(angle)).astype(np.float64)
    cos_block[np.abs(cos_block) < 1e-6] = 0.0
    sin_block[np.abs(sin_block) < 1e-6] = 0.0
    forward = np.concatenate([cos_block, -sin_block], 0)
    weight = np.where((k == 0) | (k == A), 1.0, 2.0) / PERIOD
    backward = np.concatenate([weight * cos_block, -(weight * sin_block)[1:A]], 0).T
    l = np.arange(L)[:, None]
    fwd_rows, inv_rows = [], []
    for r in range(4):
        q = r + 4 * np.arange(L)[None, :]
        angle = 2 * np.pi * (l * q % SEG) / SEG
        c, s = np.cos(angle), np.sin(angle)
        fwd_rows.append(np.block([[c, -s], [s, c]]))
        inv_rows.append(np.block([[c.T, s.T], [-s.T, c.T]]))
    j = np.arange(SEG)[None, :]
    twist = 2 * np.pi * (k * j % PERIOD) / PERIOD
    row = np.arange(512)
    column = (row // 2) % 4 * 128 + row // 8 * 2 + row % 2
    order = np.zeros((512, 512))
    order[row, column] = 1.0
    return {
        "fwd_pair": low(spread(forward, 16)),
        "fwd_one": low(spread(forward, 8)),
        "inv_pair": low(spread(backward, 16)),
        "inv_one": low(spread(backward / 256.0, 8)),
        "fwd_rows": low(np.stack(fwd_rows)),
        "inv_rows": low(np.stack(inv_rows)),
        "cos_twist": np.cos(twist).astype(np.float32),
        "sin_twist": np.sin(twist).astype(np.float32),
        "order": low(order),
    }


def mm(left, right):
    return jnp.dot(left, right, preferred_element_type=F32)


def up(value):
    return value.astype(F32)


def whole():
    return pl.BlockSpec(memory_space=pltpu.VMEM)


def pack_kernel(index_ref, q_ref, k_ref, v_ref, o_ref, f_ref, order_ref, out_ref):
    step = pl.program_id(0)
    gated = (up(k_ref[...]) * up(v_ref[...])).astype(BF)
    grad = (up(q_ref[...]) * up(o_ref[...])).astype(BF)
    both = jnp.concatenate([gated, grad], axis=0)

    def by_owner(field, half):
        columns = jnp.concatenate(
            [field[:, g * 256 + half * 128 : g * 256 + half * 128 + 128] for g in range(4)], axis=1
        )
        return lax.dot_general(
            order_ref[...], columns, (((1,), (1,)), ((), ())), preferred_element_type=F32
        )

    for half in range(2):
        rows = by_owner(both, half)
        pair = jnp.concatenate(
            [rows[:, :L].reshape(64, 8, L), rows[:, L:].reshape(64, 8, L)], axis=1
        )
        out_ref[half * 64 : half * 64 + 64, pl.ds(pl.multiple_of(step * 16, 16), 16), :] = (
            pair.astype(BF)
        )

    @pl.when(step == 0)
    def _():
        taps = f_ref[...].astype(BF)
        for half in range(2):
            rows = by_owner(taps, half).reshape(64, 8, L)
            out_ref[half * 64 : half * 64 + 64, 64:72, :] = rows.astype(BF)


def pack(index, q_in, k_in, v_in, out_grad, filters, order):
    field = pl.BlockSpec((L, 1024), lambda i, s: (i, 0))
    return pl.pallas_call(
        pack_kernel,
        out_shape=jax.ShapeDtypeStruct((DEV, ROWS, L), BF),
        grid_spec=pltpu.PrefetchScalarGridSpec(
            num_scalar_prefetch=1,
            grid=(4,),
            in_specs=[field] * 4
            + [
                pl.BlockSpec((L, 1024), lambda i, s: (s[0], 0)),
                pl.BlockSpec((512, 512), lambda i, s: (0, 0)),
            ],
            out_specs=pl.BlockSpec((DEV, ROWS, L), lambda i, s: (0, 0, 0)),
        ),
        compiler_params=pltpu.CompilerParams(vmem_limit_bytes=40 * MIB),
        name="pack",
    )(index, q_in, k_in, v_in, out_grad, filters, order)


def quarters(value):
    return [value[:, i * L : (i + 1) * L] for i in range(4)]


def butterfly(re, im, sign):
    ar, br, cr, dr = re[0] + re[2], re[0] - re[2], re[1] + re[3], re[1] - re[3]
    ai, bi, ci, di = im[0] + im[2], im[0] - im[2], im[1] + im[3], im[1] - im[3]
    plus = (br - di, bi + dr)
    minus = (br + di, bi - dr)
    first, third = (plus, minus) if sign > 0 else (minus, plus)
    return [(ar + cr, ai + ci), first, (ar - cr, ai - ci), third]


def twist_forward(sums_ref, cos_ref, sin_ref, out_ref, height):
    for k in range(KH):
        re = sums_ref[k * height : (k + 1) * height, :]
        im = sums_ref[(KH + k) * height : (KH + k + 1) * height, :]
        c = cos_ref[k : k + 1, :]
        s = sin_ref[k : k + 1, :]
        parts = butterfly(quarters(re * c + im * s), quarters(im * c - re * s), -1)
        for n, (zr, zi) in enumerate(parts):
            rows = slice(k * height, (k + 1) * height)
            out_ref[rows, n * 256 : n * 256 + L] = zr.astype(BF)
            out_ref[rows, n * 256 + L : n * 256 + 256] = zi.astype(BF)


def rows_of(data_ref, table_ref, out_ref, height):
    for n in range(4):
        cols = slice(n * 256, (n + 1) * 256)
        out_ref[: KH * height, cols] = mm(data_ref[: KH * height, cols], table_ref[n])


def twist_back(rows_ref, cos_ref, sin_ref, out_ref, height):
    for k in range(KH):
        rows = slice(k * height, (k + 1) * height)
        re = [rows_ref[rows, n * 256 : n * 256 + L] for n in range(4)]
        im = [rows_ref[rows, n * 256 + L : n * 256 + 256] for n in range(4)]
        for n, (ur, ui) in enumerate(butterfly(re, im, 1)):
            cols = slice(n * L, (n + 1) * L)
            c = cos_ref[k : k + 1, cols]
            s = sin_ref[k : k + 1, cols]
            out_ref[rows, cols] = (ur * c - ui * s).astype(BF)
            if 0 < k < A:
                lower = (KH + k - 1) * height
                out_ref[lower : lower + height, cols] = (ui * c + ur * s).astype(BF)


def transform_kernel(
    in_ref, fp_ref, fo_ref, ip_ref, io_ref, fr_ref, ir_ref, cos_ref, sin_ref, out_ref,
    sums_ref, z_ref, spec_ref, y_ref, u_ref, filt_ref, taps_ref,
):
    taps_in = jnp.concatenate(
        [up(in_ref[:, g, 64:72, :]).reshape(A * 8, L) for g in range(4)], axis=1
    ).astype(BF)
    sums_ref[: 2 * KH * 8, :] = mm(fo_ref[...], taps_in)
    twist_forward(sums_ref, cos_ref, sin_ref, z_ref, 8)
    rows_of(z_ref, fr_ref, filt_ref, 8)
    taps_ref[...] = jnp.zeros_like(taps_ref)

    def group(g, carry):
        data = jnp.concatenate(
            [in_ref[:, g, n * 16 : n * 16 + 16, :].reshape(A * 16, L) for n in range(4)], axis=1
        )
        sums_ref[...] = mm(fp_ref[...], data)
        twist_forward(sums_ref, cos_ref, sin_ref, z_ref, 16)
        rows_of(z_ref, fr_ref, spec_ref, 16)
        for k in range(KH):
            for n in range(4):
                re = slice(n * 256, n * 256 + L)
                im = slice(n * 256 + L, n * 256 + 256)
                r8 = slice(k * 8, k * 8 + 8)
                rg = slice(k * 16, k * 16 + 8)
                rr = slice(k * 16 + 8, k * 16 + 16)
                fr, fi = filt_ref[r8, re], filt_ref[r8, im]
                gr, gi = spec_ref[rg, re], spec_ref[rg, im]
                hr, hi = spec_ref[rr, re], spec_ref[rr, im]
                taps_ref[r8, re] += hr * gr + hi * gi
                taps_ref[r8, im] += hi * gr - hr * gi
                rows = slice(k * 16, k * 16 + 16)
                y_ref[rows, re] = jnp.concatenate(
                    [gr * fr - gi * fi, hr * fr + hi * fi], axis=0
                ).astype(BF)
                y_ref[rows, im] = jnp.concatenate(
                    [gr * fi + gi * fr, hi * fr - hr * fi], axis=0
                ).astype(BF)
        rows_of(y_ref, ir_ref, spec_ref, 16)
        twist_back(spec_ref, cos_ref, sin_ref, u_ref, 16)
        result = mm(ip_ref[...], u_ref[...])
        for n in range(4):
            out_ref[:, g, n * 16 : n * 16 + 16, :] = (
                result[:, n * L : (n + 1) * L].astype(BF).reshape(A, 16, L)
            )
        return carry

    lax.fori_loop(0, X, group, 0)

    y_ref[: KH * 8, :] = taps_ref[...].astype(BF)
    rows_of(y_ref, ir_ref, spec_ref, 8)
    twist_back(spec_ref, cos_ref, sin_ref, u_ref, 8)
    result = mm(io_ref[...], u_ref[: 2 * A * 8, :])
    place = lax.broadcasted_iota(jnp.int32, (A * 8, L), 0) % 8 // 2
    for g in range(4):
        total = jnp.zeros((A * 8, L), F32)
        for n in range(4):
            moved = pltpu.roll(result[:, n * L : (n + 1) * L], (2 * (n - g)) % (A * 8), 0)
            total = jnp.where(place == n, moved, total)
        out_ref[:, g, 64:72, :] = total.reshape(A, 8, L).astype(BF)


def transform(fields, t):
    pair = KH * 16
    return pl.pallas_call(
        transform_kernel,
        out_shape=jax.ShapeDtypeStruct((A, X, ROWS, L), BF),
        in_specs=[whole()] * 9,
        out_specs=whole(),
        scratch_shapes=[
            pltpu.VMEM((2 * pair, SEG), F32),
            pltpu.VMEM((pair, 2 * SEG), BF),
            pltpu.VMEM((pair, 2 * SEG), F32),
            pltpu.VMEM((pair, 2 * SEG), BF),
            pltpu.VMEM((2 * A * 16, SEG), BF),
            pltpu.VMEM((KH * 8, 2 * SEG), F32),
            pltpu.VMEM((KH * 8, 2 * SEG), F32),
        ],
        compiler_params=pltpu.CompilerParams(vmem_limit_bytes=48 * MIB),
        name="transform",
    )(
        fields, t["fwd_pair"], t["fwd_one"], t["inv_pair"], t["inv_one"],
        t["fwd_rows"], t["inv_rows"], t["cos_twist"], t["sin_twist"],
    )


def finish_kernel(
    in_ref, q_ref, k_ref, v_ref, o_ref, skip_ref, order_ref, dq_ref, dk_ref, dv_ref, df_ref
):
    step = pl.program_id(0)

    def in_place(rows):
        return lax.dot_general(
            rows.astype(BF), order_ref[...], (((0,), (0,)), ((), ())), preferred_element_type=F32
        )

    for half in range(2):
        part = up(
            in_ref[half * 64 : half * 64 + 64, pl.ds(pl.multiple_of(step * 16, 16), 16), :]
        )
        rows = jnp.concatenate(
            [part[:, :8].reshape(512, L), part[:, 8:].reshape(512, L)], axis=1
        )
        conv = in_place(rows)
        for g in range(4):
            cols = slice(g * 256 + half * 128, g * 256 + half * 128 + 128)
            state = conv[:L, g * L : (g + 1) * L]
            back = conv[L:, g * L : (g + 1) * L]
            q, k, v, o = (up(ref[:, cols]) for ref in (q_ref, k_ref, v_ref, o_ref))
            skip = skip_ref[:, cols]
            mixed = state + skip * up((k * v).astype(BF))
            total = back + skip * up((q * o).astype(BF))
            dq_ref[:, cols] = (o * mixed).astype(BF)
            dk_ref[:, cols] = (total * v).astype(BF)
            dv_ref[:, cols] = (total * k).astype(BF)

    @pl.when(step == 0)
    def _():
        for half in range(2):
            rows = up(in_ref[half * 64 : half * 64 + 64, 64:72, :]).reshape(512, L)
            taps = in_place(rows)
            for n in range(4):
                df_ref[n * L : (n + 1) * L, half * 128 : half * 128 + 128] = taps[
                    :, n * L : (n + 1) * L
                ]


def finish(fields, q_in, k_in, v_in, out_grad, skip, order):
    field = pl.BlockSpec((L, 1024), lambda i: (i, 0))
    return pl.pallas_call(
        finish_kernel,
        out_shape=(
            jax.ShapeDtypeStruct((SEG, 1024), BF),
            jax.ShapeDtypeStruct((SEG, 1024), BF),
            jax.ShapeDtypeStruct((SEG, 1024), BF),
            jax.ShapeDtypeStruct((SEG, 256), F32),
        ),
        grid=(4,),
        in_specs=[pl.BlockSpec((DEV, ROWS, L), lambda i: (0, 0, 0))]
        + [field] * 4
        + [
            pl.BlockSpec((1, 1024), lambda i: (0, 0)),
            pl.BlockSpec((512, 512), lambda i: (0, 0)),
        ],
        out_specs=(field, field, field, pl.BlockSpec((SEG, 256), lambda i: (0, 0))),
        compiler_params=pltpu.CompilerParams(vmem_limit_bytes=40 * MIB),
        name="finish",
    )(fields, q_in, k_in, v_in, out_grad, skip, order)


def body(q_in, k_in, v_in, out_grad, filters, skip):
    t = {name: jnp.asarray(value) for name, value in constants().items()}
    index = lax.axis_index("ch").astype(jnp.int32).reshape(1)
    sent = pack(index, q_in, k_in, v_in, out_grad, filters, t["order"])
    columns = lax.all_to_all(sent, ("ctx", "ch"), split_axis=0, concat_axis=0, tiled=True)
    results = transform(columns.reshape(A, X, ROWS, L), t)
    blocks = lax.all_to_all(
        results.reshape(DEV, ROWS, L), ("ctx", "ch"), split_axis=0, concat_axis=0, tiled=True
    )
    return finish(blocks, q_in, k_in, v_in, out_grad, skip.reshape(1, 1024), t["order"])


def solution(mesh):
    return jax.shard_map(
        body,
        mesh=mesh,
        in_specs=(
            P("ctx", "ch"),
            P("ctx", "ch"),
            P("ctx", "ch"),
            P("ctx", "ch"),
            P("ctx", None),
            P("ch"),
        ),
        out_specs=(P("ctx", "ch"), P("ctx", "ch"), P("ctx", "ch"), P("ctx", "ch")),
        check_vma=False,
    )
```

time: 472 us -> 116 us (0.25); the launches traced: 463 us -> 115 us
  matrix products: 252 us -> 0 us
  blocking collectives: 0 us -> 83.4 us
  waiting for transfers between devices: 60.8 us -> 0 us
  local copies, waits for them, and re-layouts: 62.5 us -> 7.61 us
  starting transfers between devices: 44.3 us -> 0 us
  other arithmetic: 28 us -> 0 us
  Pallas kernels: 0 us -> 23.4 us
  between operations: 15.1 us -> 0.81 us
    dot_general x36 -> x0, matrix products: 252 us -> none  [the longest x30 185 us: multiply(): jnp.einsum(form, table.astype(jnp.bfloat16), data, preferred_element_type...]
    all_to_all x0 -> x2, blocking collectives: none -> 83.4 us  [the longest x1 45.1 us: body(): lax.all_to_all(sent, ('ctx', 'ch'), split_axis=0, concat_axis=0, tiled=True)]
    all_to_all x6 -> x0, waiting for transfers between devices: 60.8 us -> none  [the longest x1 24.6 us: body(): lax.all_to_all(state_blk, 'ctx', split_axis=0, concat_axis=2, tiled=True)]
    all_to_all x6 -> x0, starting transfers between devices: 43.9 us -> none  [the longest x1 9.93 us: body(): lax.all_to_all(regroup(gated_low), 'ctx', split_axis=2, concat_axis=0, ti...]
    unnamed x71 -> x40, local copies, waits for them, and re-layouts: 39.7 us -> 7.61 us
    pallas_call x0 -> x3, Pallas kernels: none -> 23.4 us  [the longest x1 17 us: transform(): pl.pallas_call(transform_kernel, out_shape=jax.ShapeDtypeStruct((A, X, RO...]
    unnamed x3 -> x0, other arithmetic: 23.1 us -> none
    transpose x6 -> x0, local copies, waits for them, and re-layouts: 8.79 us -> none  [the longest x3 8.45 us: ungroup(): return field.reshape(seq_rows, ctx_count, ch_count, narrow).transpose(0,...]
  transfers between devices with their start and end apart: 7 -> 0, of which waited for: 5 -> 0; matrix products, arithmetic and copies ran while one was open for 18% -> 0% of each run, Pallas kernels for 0% -> 0%
where the time goes in v1:
time: 116 us; the launch traced here: 115 us
  blocking collectives  83.4 us (72%)
  Pallas kernels  23.4 us (20%)
  local copies, waits for them, and re-layouts  7.61 us (7%)
    all_to_all x1, blocking collectives, body(): lax.all_to_all(sent, ('ctx', 'ch'), split_axis=0, concat_axis=0, tiled=True)  45.1 us
    all_to_all x1, blocking collectives, body(): lax.all_to_all(results.reshape(DEV, ROWS, L), ('ctx', 'ch'), split_axis=0...  38.4 us
    pallas_call x1, Pallas kernels, transform(): pl.pallas_call(transform_kernel, out_shape=jax.ShapeDtypeStruct((A, X, RO...  17 us
    unnamed x40, local copies, waits for them, and re-layouts  7.61 us
    pallas_call x1, Pallas kernels, finish(): pl.pallas_call(finish_kernel, out_shape=(jax.ShapeDtypeStruct((SEG, 1024)...  4.06 us
    pallas_call x1, Pallas kernels, pack(): pl.pallas_call(pack_kernel, out_shape=jax.ShapeDtypeStruct((DEV, ROWS, L)...  2.39 us

profile of v1, /device:TPU:1, one launch (start us, length us, event | category | flops | bytes accessed | tf_op | source)
XLA Modules:
  0.0 115.3 jit_solution(9634753798941846091)
XLA Ops:
  0.6 0.0 copy-start
  0.6 1.2 %copy-done = bf16[512,1024]{1,0:T(8,128)(2,1)S(1)} copy-done((bf16[512,1024]{1,0:T(8,128)(2,1)S(1)}, bf16[512,1024]{1,0:T(8,128)(2,1)}, u32[]{:S(2)}) %copy-start) | copy-done | bytes 1048600
  1.9 1.2 %copy-done.2 = bf16[512,1024]{1,0:T(8,128)(2,1)S(1)} copy-done((bf16[512,1024]{1,0:T(8,128)(2,1)S(1)}, bf16[512,1024]{1,0:T(8,128)(2,1)}, u32[]{:S(2)}) %copy-start.2) | copy-done | bytes 1048600
  3.1 1.2 %copy-done.4 = bf16[512,1024]{1,0:T(8,128)(2,1)S(1)} copy-done((bf16[512,1024]{1,0:T(8,128)(2,1)S(1)}, bf16[512,1024]{1,0:T(8,128)(2,1)}, u32[]{:S(2)}) %copy-start.4) | copy-done | bytes 1048600
  4.3 1.2 %copy-done.6 = bf16[512,1024]{1,0:T(8,128)(2,1)S(1)} copy-done((bf16[512,1024]{1,0:T(8,128)(2,1)S(1)}, bf16[512,1024]{1,0:T(8,128)(2,1)}, u32[]{:S(2)}) %copy-start.6) | copy-done | bytes 1048600
  5.5 1.0 copy-done.8
  6.6 1.6 %copy-done.10 = f32[512,1024]{1,0:T(8,128)S(1)} copy-done((f32[512,1024]{1,0:T(8,128)S(1)}, f32[512,1024]{1,0:T(8,128)}, u32[]{:S(2)}) %copy-start.10) | copy-done | bytes 2097176
  8.2 2.4 %pack.1 = bf16[128,72,128]{2,1,0:T(8,128)(2,1)S(1)} custom-call(s32[1]{0:T(128)} %bitcast.index_ref, bf16[512,1024]{1,0:T(8,128)(2,1)S(1)} %copy-done, bf16[512,1024]{1,0:T(8,128)(2,1)S(1)} %copy-done.2, bf16[512,1024]{1,0:T(8,128)(2,1)S(1)} %copy-done.4, bf16[512,1024]{1,0:T(8,128)(2,1)S(1)} %copy-done.6, f32[512,1024]{1,0:T(8,128)S(1)} %copy-done.10, ...), custom_call_target="tpu_custom_call" | custom-call | tf_op jit(solution)/shard_map/pack/pallas_call | solution.py:119
  10.6 0.0 copy-start.11
  10.6 0.0 copy-start.12
  10.6 0.0 copy-start.13
  10.6 0.0 copy-start.14
  10.6 0.0 copy-start.15
  10.6 0.0 copy-start.16
  10.6 0.0 copy-start.17
  10.7 0.0 copy-start.18
  10.7 45.1 %all_to_all.10 = bf16[128,72,128]{2,1,0:T(8,128)(2,1)} all-to-all(bf16[128,72,128]{2,1,0:T(8,128)(2,1)S(1)} %pack.1), channel_id=1, replica_groups=mesh['ctx'=32,'ch'=4] {'ctx','ch'}, dimensions={0} | all-to-all | bytes 4718592 | tf_op jit(solution)/shard_map/all_to_all | solution.py:338
  55.7 0.0 copy-done.11
  55.8 0.0 copy-start.19
  55.8 17.0 %transform.1 = bf16[32,4,72,128]{3,2,1,0:T(8,128)(2,1)} custom-call(bf16[32,4,72,128]{3,2,1,0:T(8,128)(2,1)} %bitcast.5, bf16[1056,512]{1,0:T(8,128)(2,1)S(1)} %copy-done.11, bf16[528,256]{1,0:T(8,128)(2,1)S(1)} %copy-done.15, bf16[512,1024]{1,0:T(8,128)(2,1)S(1)} %copy-done.12, bf16[256,512]{1,0:T(8,128)(2,1)S(1)} %copy-done.16, ...), custom_call_target="tpu_custom_call" | custom-call | tf_op jit(solution)/shard_map/transform/pallas_call | solution.py:248
  72.8 0.0 copy-start.9
  72.8 38.4 %all_to_all.11.in_ref = bf16[128,72,128]{2,1,0:T(8,128)(2,1)S(1)} all-to-all(bf16[128,72,128]{2,1,0:T(8,128)(2,1)} %bitcast.6), channel_id=1, replica_groups=mesh['ctx'=32,'ch'=4] {'ctx','ch'}, dimensions={0} | all-to-all | bytes 4718592 | tf_op jit(solution)/shard_map/all_to_all | solution.py:340
  111.2 0.0 copy-done.19
  111.2 4.1 %finish.1 = (bf16[512,1024]{1,0:T(8,128)(2,1)}, bf16[512,1024]{1,0:T(8,128)(2,1)}, bf16[512,1024]{1,0:T(8,128)(2,1)}, f32[512,256]{1,0:T(8,128)}) custom-call(bf16[128,72,128]{2,1,0:T(8,128)(2,1)S(1)} %all_to_all.11.in_ref, bf16[512,1024]{1,0:T(8,128)(2,1)S(1)} %copy-done.1, bf16[512,1024]{1,0:T(8,128)(2,1)S(1)} %copy-done.3, ...), custom_call_target="tpu_custom_call" | custom-call | tf_op jit(solution)/shard_map/finish/pallas_call | solution.py:313
  (21 shorter events, 0.0 us)
Async XLA Ops:
  0.6 1.2 %copy-start = (bf16[512,1024]{1,0:T(8,128)(2,1)S(1)}, bf16[512,1024]{1,0:T(8,128)(2,1)}, u32[]{:S(2)}) copy-start(bf16[512,1024]{1,0:T(8,128)(2,1)} %q_ref.3) | copy-start | bytes 3145732
  1.9 1.2 %copy-start.2 = (bf16[512,1024]{1,0:T(8,128)(2,1)S(1)}, bf16[512,1024]{1,0:T(8,128)(2,1)}, u32[]{:S(2)}) copy-start(bf16[512,1024]{1,0:T(8,128)(2,1)} %k_ref.3) | copy-start | bytes 3145732
  3.1 1.2 %copy-start.4 = (bf16[512,1024]{1,0:T(8,128)(2,1)S(1)}, bf16[512,1024]{1,0:T(8,128)(2,1)}, u32[]{:S(2)}) copy-start(bf16[512,1024]{1,0:T(8,128)(2,1)} %v_ref.3) | copy-start | bytes 3145732
  4.3 1.2 %copy-start.6 = (bf16[512,1024]{1,0:T(8,128)(2,1)S(1)}, bf16[512,1024]{1,0:T(8,128)(2,1)}, u32[]{:S(2)}) copy-start(bf16[512,1024]{1,0:T(8,128)(2,1)} %o_ref.3) | copy-start | bytes 3145732
  5.5 1.0 copy-start.8
  6.6 1.6 %copy-start.10 = (f32[512,1024]{1,0:T(8,128)S(1)}, f32[512,1024]{1,0:T(8,128)}, u32[]{:S(2)}) copy-start(f32[512,1024]{1,0:T(8,128)} %f_ref.1) | copy-start | bytes 6291460
  10.6 45.2 %copy-start.11 = (bf16[1056,512]{1,0:T(8,128)(2,1)S(1)}, bf16[1056,512]{1,0:T(8,128)(2,1)}, u32[]{:S(2)}) copy-start(bf16[1056,512]{1,0:T(8,128)(2,1)} %constant.22.clone.fp_ref) | copy-start | bytes 3244036
  10.6 45.1 %copy-start.12 = (bf16[512,1024]{1,0:T(8,128)(2,1)S(1)}, bf16[512,1024]{1,0:T(8,128)(2,1)}, u32[]{:S(2)}) copy-start(bf16[512,1024]{1,0:T(8,128)(2,1)} %constant.24.clone.ip_ref) | copy-start | bytes 3145732
  10.6 45.1 %copy-start.13 = (bf16[4,256,256]{2,1,0:T(8,128)(2,1)S(1)}, bf16[4,256,256]{2,1,0:T(8,128)(2,1)}, u32[]{:S(2)}) copy-start(bf16[4,256,256]{2,1,0:T(8,128)(2,1)} %constant.27.clone.ir_ref) | copy-start | bytes 1572868
  10.6 45.1 %copy-start.14 = (bf16[4,256,256]{2,1,0:T(8,128)(2,1)S(1)}, bf16[4,256,256]{2,1,0:T(8,128)(2,1)}, u32[]{:S(2)}) copy-start(bf16[4,256,256]{2,1,0:T(8,128)(2,1)} %constant.26.clone.fr_ref) | copy-start | bytes 1572868
  10.6 45.1 %copy-start.15 = (bf16[528,256]{1,0:T(8,128)(2,1)S(1)}, bf16[528,256]{1,0:T(8,128)(2,1)}, u32[]{:S(2)}) copy-start(bf16[528,256]{1,0:T(8,128)(2,1)} %constant.23.clone.fo_ref) | copy-start | bytes 811012
  10.6 45.1 %copy-start.16 = (bf16[256,512]{1,0:T(8,128)(2,1)S(1)}, bf16[256,512]{1,0:T(8,128)(2,1)}, u32[]{:S(2)}) copy-start(bf16[256,512]{1,0:T(8,128)(2,1)} %constant.25.clone.io_ref) | copy-start | bytes 786436
  10.6 45.1 %copy-start.17 = (f32[33,512]{1,0:T(8,128)S(1)}, f32[33,512]{1,0:T(8,128)}, u32[]{:S(2)}) copy-start(f32[33,512]{1,0:T(8,128)} %constant.29.clone.sin_ref) | copy-start | bytes 202756
  10.7 45.1 %copy-start.18 = (f32[33,512]{1,0:T(8,128)S(1)}, f32[33,512]{1,0:T(8,128)}, u32[]{:S(2)}) copy-start(f32[33,512]{1,0:T(8,128)} %constant.28.clone.cos_ref) | copy-start | bytes 202756
  55.8 55.4 %copy-start.19 = (f32[1024]{0:T(1024)S(1)}, f32[1024]{0:T(1024)}, u32[]{:S(2)}) copy-start(f32[1024]{0:T(1024)} %param.20) | copy-start | bytes 12292
  72.8 38.4 %copy-start.1 = (bf16[512,1024]{1,0:T(8,128)(2,1)S(1)}, bf16[512,1024]{1,0:T(8,128)(2,1)}, u32[]{:S(2)}) copy-start(bf16[512,1024]{1,0:T(8,128)(2,1)} %q_ref.3) | copy-start | bytes 3145732
  72.8 38.4 %copy-start.3 = (bf16[512,1024]{1,0:T(8,128)(2,1)S(1)}, bf16[512,1024]{1,0:T(8,128)(2,1)}, u32[]{:S(2)}) copy-start(bf16[512,1024]{1,0:T(8,128)(2,1)} %k_ref.3) | copy-start | bytes 3145732
  72.8 38.4 %copy-start.5 = (bf16[512,1024]{1,0:T(8,128)(2,1)S(1)}, bf16[512,1024]{1,0:T(8,128)(2,1)}, u32[]{:S(2)}) copy-start(bf16[512,1024]{1,0:T(8,128)(2,1)} %v_ref.3) | copy-start | bytes 3145732
  72.8 38.4 %copy-start.7 = (bf16[512,1024]{1,0:T(8,128)(2,1)S(1)}, bf16[512,1024]{1,0:T(8,128)(2,1)}, u32[]{:S(2)}) copy-start(bf16[512,1024]{1,0:T(8,128)(2,1)} %o_ref.3) | copy-start | bytes 3145732
  72.8 38.4 %copy-start.9 = (bf16[512,512]{1,0:T(8,128)(2,1)S(1)}, bf16[512,512]{1,0:T(8,128)(2,1)}, u32[]{:S(2)}) copy-start(bf16[512,512]{1,0:T(8,128)(2,1)} %constant.30.clone.order_ref) | copy-start | bytes 1572868

commit v2 on v1

--- a/solution.py
+++ b/solution.py
@@ -59,10 +59,8 @@
     order = np.zeros((512, 512))
     order[row, column] = 1.0
     return {
-        "fwd_pair": low(spread(forward, 16)),
-        "fwd_one": low(spread(forward, 8)),
-        "inv_pair": low(spread(backward, 16)),
-        "inv_one": low(spread(backward / 256.0, 8)),
+        "forward": low(spread(forward, 8)),
+        "backward": low(spread(backward, 8)),
         "fwd_rows": low(np.stack(fwd_rows)),
         "inv_rows": low(np.stack(inv_rows)),
         "cos_twist": np.cos(twist).astype(np.float32),
@@ -83,11 +81,36 @@
     return pl.BlockSpec(memory_space=pltpu.VMEM)
 
 
-def pack_kernel(index_ref, q_ref, k_ref, v_ref, o_ref, f_ref, order_ref, out_ref):
+def pack_kernel(
+    index_ref, q_hbm, k_hbm, v_hbm, o_hbm, f_hbm, order_hbm, out_ref,
+    fields_ref, taps_ref, order_ref, field_sems, other_sems,
+):
     step = pl.program_id(0)
-    gated = (up(k_ref[...]) * up(v_ref[...])).astype(BF)
-    grad = (up(q_ref[...]) * up(o_ref[...])).astype(BF)
-    both = jnp.concatenate([gated, grad], axis=0)
+    sources = (k_hbm, v_hbm, q_hbm, o_hbm)
+
+    def field_copy(i, n):
+        rows = pl.ds(pl.multiple_of(n * L, L), L)
+        return pltpu.make_async_copy(
+            sources[i].at[rows], fields_ref.at[i, rows], field_sems.at[n, i]
+        )
+
+    def taps_copy():
+        rows = pl.ds(pl.multiple_of(index_ref[0] * L, L), L)
+        return pltpu.make_async_copy(f_hbm.at[rows], taps_ref, other_sems.at[0])
+
+    def order_copy():
+        return pltpu.make_async_copy(order_hbm, order_ref, other_sems.at[1])
+
+    @pl.when(step == 0)
+    def _():
+        for i in range(4):
+            field_copy(i, 0).start()
+        order_copy().start()
+        for n in range(1, 4):
+            for i in range(4):
+                field_copy(i, n).start()
+        taps_copy().start()
+        order_copy().wait()
 
     def by_owner(field, half):
         columns = jnp.concatenate(
@@ -97,39 +120,47 @@
             order_ref[...], columns, (((1,), (1,)), ((), ())), preferred_element_type=F32
         )
 
-    for half in range(2):
-        rows = by_owner(both, half)
-        pair = jnp.concatenate(
-            [rows[:, :L].reshape(64, 8, L), rows[:, L:].reshape(64, 8, L)], axis=1
-        )
-        out_ref[half * 64 : half * 64 + 64, pl.ds(pl.multiple_of(step * 16, 16), 16), :] = (
-            pair.astype(BF)
-        )
-
-    @pl.when(step == 0)
+    @pl.when(step < 4)
     def _():
-        taps = f_ref[...].astype(BF)
+        for i in range(4):
+            field_copy(i, step).wait()
+        rows = pl.ds(pl.multiple_of(step * L, L), L)
+        k, v, q, o = (up(fields_ref[i, rows, :]) for i in range(4))
+        both = jnp.concatenate([(k * v).astype(BF), (q * o).astype(BF)], axis=0)
         for half in range(2):
-            rows = by_owner(taps, half).reshape(64, 8, L)
-            out_ref[half * 64 : half * 64 + 64, 64:72, :] = rows.astype(BF)
+            moved = by_owner(both, half)
+            pair = jnp.concatenate(
+                [moved[:, :L].reshape(64, 8, L), moved[:, L:].reshape(64, 8, L)], axis=1
+            )
+            out_ref[half * 64 : half * 64 + 64, :, :] = pair.astype(BF)
+
+    @pl.when(step == 4)
+    def _():
+        taps_copy().wait()
+        taps = taps_ref[...].astype(BF)
+        for half in range(2):
+            moved = by_owner(taps, half).reshape(64, 8, L)
+            out_ref[half * 64 : half * 64 + 64, :8, :] = moved.astype(BF)
 
 
 def pack(index, q_in, k_in, v_in, out_grad, filters, order):
-    field = pl.BlockSpec((L, 1024), lambda i, s: (i, 0))
     return pl.pallas_call(
         pack_kernel,
         out_shape=jax.ShapeDtypeStruct((DEV, ROWS, L), BF),
         grid_spec=pltpu.PrefetchScalarGridSpec(
             num_scalar_prefetch=1,
-            grid=(4,),
-            in_specs=[field] * 4
-            + [
-                pl.BlockSpec((L, 1024), lambda i, s: (s[0], 0)),
-                pl.BlockSpec((512, 512), lambda i, s: (0, 0)),
+            grid=(5,),
+            in_specs=[pl.BlockSpec(memory_space=pl.ANY)] * 6,
+            out_specs=pl.BlockSpec((DEV, 16, L), lambda i, s: (0, i, 0)),
+            scratch_shapes=[
+                pltpu.VMEM((4, SEG, 1024), BF),
+                pltpu.VMEM((L, 1024), F32),
+                pltpu.VMEM((512, 512), BF),
+                pltpu.SemaphoreType.DMA((4, 4)),
+                pltpu.SemaphoreType.DMA((2,)),
             ],
-            out_specs=pl.BlockSpec((DEV, ROWS, L), lambda i, s: (0, 0, 0)),
         ),
-        compiler_params=pltpu.CompilerParams(vmem_limit_bytes=40 * MIB),
+        compiler_params=pltpu.CompilerParams(vmem_limit_bytes=60 * MIB),
         name="pack",
     )(index, q_in, k_in, v_in, out_grad, filters, order)
 
@@ -147,123 +178,223 @@
     return [(ar + cr, ai + ci), first, (ar - cr, ai - ci), third]
 
 
-def twist_forward(sums_ref, cos_ref, sin_ref, out_ref, height):
-    for k in range(KH):
-        re = sums_ref[k * height : (k + 1) * height, :]
-        im = sums_ref[(KH + k) * height : (KH + k + 1) * height, :]
-        c = cos_ref[k : k + 1, :]
-        s = sin_ref[k : k + 1, :]
+def twist_forward(fields, cos_ref, sin_ref, k):
+    c = cos_ref[k : k + 1, :]
+    s = sin_ref[k : k + 1, :]
+    found = []
+    for sums_ref in fields:
+        re = sums_ref[k * 8 : k * 8 + 8, :]
+        im = sums_ref[(KH + k) * 8 : (KH + k) * 8 + 8, :]
         parts = butterfly(quarters(re * c + im * s), quarters(im * c - re * s), -1)
-        for n, (zr, zi) in enumerate(parts):
-            rows = slice(k * height, (k + 1) * height)
-            out_ref[rows, n * 256 : n * 256 + L] = zr.astype(BF)
-            out_ref[rows, n * 256 + L : n * 256 + 256] = zi.astype(BF)
-
-
-def rows_of(data_ref, table_ref, out_ref, height):
-    for n in range(4):
-        cols = slice(n * 256, (n + 1) * 256)
-        out_ref[: KH * height, cols] = mm(data_ref[: KH * height, cols], table_ref[n])
-
-
-def twist_back(rows_ref, cos_ref, sin_ref, out_ref, height):
-    for k in range(KH):
-        rows = slice(k * height, (k + 1) * height)
-        re = [rows_ref[rows, n * 256 : n * 256 + L] for n in range(4)]
-        im = [rows_ref[rows, n * 256 + L : n * 256 + 256] for n in range(4)]
-        for n, (ur, ui) in enumerate(butterfly(re, im, 1)):
-            cols = slice(n * L, (n + 1) * L)
-            c = cos_ref[k : k + 1, cols]
-            s = sin_ref[k : k + 1, cols]
-            out_ref[rows, cols] = (ur * c - ui * s).astype(BF)
-            if 0 < k < A:
-                lower = (KH + k - 1) * height
-                out_ref[lower : lower + height, cols] = (ui * c + ur * s).astype(BF)
+        found.append(jnp.concatenate([part for pair in parts for part in pair], axis=1))
+    return found
+
+
+def store_rows(ref, row, pieces):
+    ref[row : row + 8 * len(pieces), :] = jnp.concatenate(pieces, axis=0).astype(BF)
+
+
+def twist_back(rows_ref, cos_ref, sin_ref, row, k):
+    re = [rows_ref[row : row + 8, n * 256 : n * 256 + L] for n in range(4)]
+    im = [rows_ref[row : row + 8, n * 256 + L : n * 256 + 256] for n in range(4)]
+    real, imag = [], []
+    for n, (ur, ui) in enumerate(butterfly(re, im, 1)):
+        c = cos_ref[k : k + 1, n * L : (n + 1) * L]
+        s = sin_ref[k : k + 1, n * L : (n + 1) * L]
+        real.append(ur * c - ui * s)
+        imag.append(ui * c + ur * s)
+    return jnp.concatenate(real, axis=1), jnp.concatenate(imag, axis=1)
+
+
+def interleave(first, second):
+    n, m = len(first), len(second)
+    if n == 0 or m == 0:
+        order = list(first) + list(second)
+    else:
+        order = []
+        done = 0
+        for i, piece in enumerate(first):
+            order.append(piece)
+            upto = (i + 1) * m // n
+            order.extend(second[done:upto])
+            done = upto
+    for piece in order:
+        piece()
+
+
+PAIRS = [(0, 1, A)] + [(k, k + 1) for k in range(2, A, 2)]
 
 
 def transform_kernel(
-    in_ref, fp_ref, fo_ref, ip_ref, io_ref, fr_ref, ir_ref, cos_ref, sin_ref, out_ref,
-    sums_ref, z_ref, spec_ref, y_ref, u_ref, filt_ref, taps_ref,
+    in_ref, fwd_ref, inv_ref, fr_ref, ir_ref, cos_ref, sin_ref, out_ref,
+    sums_ref, z_ref, spec_ref, y_ref, v_ref, u_ref, filt_sums, filt_z, filt_ref, taps_ref,
 ):
-    taps_in = jnp.concatenate(
-        [up(in_ref[:, g, 64:72, :]).reshape(A * 8, L) for g in range(4)], axis=1
-    ).astype(BF)
-    sums_ref[: 2 * KH * 8, :] = mm(fo_ref[...], taps_in)
-    twist_forward(sums_ref, cos_ref, sin_ref, z_ref, 8)
-    rows_of(z_ref, fr_ref, filt_ref, 8)
-    taps_ref[...] = jnp.zeros_like(taps_ref)
-
-    def group(g, carry):
-        data = jnp.concatenate(
-            [in_ref[:, g, n * 16 : n * 16 + 16, :].reshape(A * 16, L) for n in range(4)], axis=1
-        )
-        sums_ref[...] = mm(fp_ref[...], data)
-        twist_forward(sums_ref, cos_ref, sin_ref, z_ref, 16)
-        rows_of(z_ref, fr_ref, spec_ref, 16)
-        for k in range(KH):
+    def load(g, n, field):
+        rows = up(in_ref[:, g, n * 16 : n * 16 + 16, :])
+        return rows[:, field * 8 : field * 8 + 8].reshape(A * 8, L).astype(BF)
+
+    def block_sums(g):
+        def piece(field, half):
+            data = jnp.concatenate([load(g, 2 * half + i, field) for i in range(2)], axis=1)
+            sums_ref[g % 2, field, :, half * 256 : half * 256 + 256] = mm(fwd_ref[...], data)
+
+        return [lambda f=f, h=h: piece(f, h) for f in range(2) for h in range(2)]
+
+    def forward_twist(g):
+        def piece(k):
+            fields = [sums_ref.at[g % 2, 0], sums_ref.at[g % 2, 1]]
+            store_rows(z_ref.at[g % 2], k * 16, twist_forward(fields, cos_ref, sin_ref, k))
+
+        return [lambda k=k: piece(k) for k in range(KH)]
+
+    def row_sums(data, table, out):
+        def piece(n):
+            cols = slice(n * 256, (n + 1) * 256)
+            out[:, cols] = mm(data[:, cols], table[n])
+
+        return [lambda n=n: piece(n) for n in range(4)]
+
+    def products(g):
+        def piece(k):
+            spec, y = spec_ref.at[g % 2], y_ref.at[g % 2]
+            r8 = slice(k * 8, k * 8 + 8)
+            rg = slice(k * 16, k * 16 + 8)
+            rr = slice(k * 16 + 8, k * 16 + 16)
             for n in range(4):
                 re = slice(n * 256, n * 256 + L)
                 im = slice(n * 256 + L, n * 256 + 256)
-                r8 = slice(k * 8, k * 8 + 8)
-                rg = slice(k * 16, k * 16 + 8)
-                rr = slice(k * 16 + 8, k * 16 + 16)
                 fr, fi = filt_ref[r8, re], filt_ref[r8, im]
-                gr, gi = spec_ref[rg, re], spec_ref[rg, im]
-                hr, hi = spec_ref[rr, re], spec_ref[rr, im]
-                taps_ref[r8, re] += hr * gr + hi * gi
-                taps_ref[r8, im] += hi * gr - hr * gi
+                gr, gi = spec[rg, re], spec[rg, im]
+                hr, hi = spec[rr, re], spec[rr, im]
+                wr = hr * gr + hi * gi
+                wi = hi * gr - hr * gi
+                if g > 0:
+                    wr = wr + taps_ref[r8, re]
+                    wi = wi + taps_ref[r8, im]
+                taps_ref[r8, re] = wr
+                taps_ref[r8, im] = wi
                 rows = slice(k * 16, k * 16 + 16)
-                y_ref[rows, re] = jnp.concatenate(
+                y[rows, re] = jnp.concatenate(
                     [gr * fr - gi * fi, hr * fr + hi * fi], axis=0
                 ).astype(BF)
-                y_ref[rows, im] = jnp.concatenate(
+                y[rows, im] = jnp.concatenate(
                     [gr * fi + gi * fr, hi * fr - hr * fi], axis=0
                 ).astype(BF)
-        rows_of(y_ref, ir_ref, spec_ref, 16)
-        twist_back(spec_ref, cos_ref, sin_ref, u_ref, 16)
-        result = mm(ip_ref[...], u_ref[...])
-        for n in range(4):
-            out_ref[:, g, n * 16 : n * 16 + 16, :] = (
-                result[:, n * L : (n + 1) * L].astype(BF).reshape(A, 16, L)
+
+        return [lambda k=k: piece(k) for k in range(KH)]
+
+    def back_twist(rows, place, out):
+        def piece(ks):
+            parts = [twist_back(rows, cos_ref, sin_ref, place(k), k) for k in ks]
+            store_rows(out, ks[0] * 8, [parts[0][0], parts[1][0]])
+            if len(ks) == 3:
+                store_rows(out, A * 8, [parts[2][0], parts[1][1]])
+            else:
+                store_rows(out, (A + ks[0]) * 8, [parts[0][1], parts[1][1]])
+
+        return [lambda ks=ks: piece(ks) for ks in PAIRS]
+
+    def results(g):
+        def piece(half):
+            cols = slice(half * 256, half * 256 + 256)
+            state = mm(inv_ref[...], u_ref[g % 2, 0, :, cols]).reshape(A, 8, 256)
+            back = mm(inv_ref[...], u_ref[g % 2, 1, :, cols]).reshape(A, 8, 256)
+            both = jnp.concatenate([state, back], axis=1).astype(BF)
+            for i in range(2):
+                n = 2 * half + i
+                out_ref[:, g, n * 16 : n * 16 + 16, :] = both[:, :, i * L : (i + 1) * L]
+
+        return [lambda h=h: piece(h) for h in range(2)]
+
+    def forward_rows(g):
+        return row_sums(z_ref.at[g % 2], fr_ref, spec_ref.at[g % 2])
+
+    def back_rows(g):
+        return row_sums(y_ref.at[g % 2], ir_ref, v_ref.at[g % 2])
+
+    def back_twists(g):
+        pieces = []
+        for f in range(2):
+            pieces += back_twist(
+                v_ref.at[g % 2], lambda k, f=f: k * 16 + f * 8, u_ref.at[g % 2, f]
             )
-        return carry
-
-    lax.fori_loop(0, X, group, 0)
-
-    y_ref[: KH * 8, :] = taps_ref[...].astype(BF)
-    rows_of(y_ref, ir_ref, spec_ref, 8)
-    twist_back(spec_ref, cos_ref, sin_ref, u_ref, 8)
-    result = mm(io_ref[...], u_ref[: 2 * A * 8, :])
+        return pieces
+
+    def filter_sums():
+        def piece(half):
+            data = jnp.concatenate(
+                [
+                    up(in_ref[:, 2 * half + i, 64:72, :]).reshape(A * 8, L).astype(BF)
+                    for i in range(2)
+                ],
+                axis=1,
+            )
+            filt_sums[:, half * 256 : half * 256 + 256] = mm(fwd_ref[...], data)
+
+        return [lambda h=h: piece(h) for h in range(2)]
+
+    def filter_twist():
+        def piece(ks):
+            found = [twist_forward([filt_sums], cos_ref, sin_ref, k)[0] for k in ks]
+            store_rows(filt_z, ks[0] * 8, found)
+
+        return [lambda ks=ks: piece(ks) for ks in [(k, k + 1) for k in range(0, A, 2)] + [(A,)]]
+
+    def taps_rows():
+        def piece(k):
+            filt_z[k * 8 : k * 8 + 16, :] = taps_ref[k * 8 : k * 8 + 16, :].astype(BF)
+
+        def last():
+            filt_z[A * 8 :, :] = taps_ref[A * 8 :, :].astype(BF)
+
+        return [lambda k=k: piece(k) for k in range(0, A, 2)] + [last]
+
+    interleave(filter_sums() + block_sums(0), [])
+    interleave(block_sums(1)[:2], filter_twist())
+    interleave(row_sums(filt_z, fr_ref, filt_ref) + block_sums(1)[2:], forward_twist(0))
+    for g in range(X):
+        interleave(forward_rows(g), back_twists(g - 1) if g > 0 else [])
+        interleave(results(g - 1) if g > 0 else [], products(g))
+        interleave(back_rows(g), forward_twist(g + 1) if g + 1 < X else taps_rows())
+        if g + 2 < X:
+            interleave(block_sums(g + 2), [])
+    interleave(row_sums(filt_z, ir_ref, filt_ref), back_twists(X - 1))
+    interleave(results(X - 1), back_twist(filt_ref, lambda k: k * 8, u_ref.at[0, 0]))
+
+    result = mm(inv_ref[...], u_ref[0, 0]) * (1.0 / 256.0)
     place = lax.broadcasted_iota(jnp.int32, (A * 8, L), 0) % 8 // 2
     for g in range(4):
-        total = jnp.zeros((A * 8, L), F32)
-        for n in range(4):
-            moved = pltpu.roll(result[:, n * L : (n + 1) * L], (2 * (n - g)) % (A * 8), 0)
+        total = result[:, :L] if g == 0 else pltpu.roll(result[:, :L], (-2 * g) % (A * 8), 0)
+        for n in range(1, 4):
+            part = result[:, n * L : (n + 1) * L]
+            moved = part if n == g else pltpu.roll(part, (2 * (n - g)) % (A * 8), 0)
             total = jnp.where(place == n, moved, total)
         out_ref[:, g, 64:72, :] = total.reshape(A, 8, L).astype(BF)
 
 
 def transform(fields, t):
-    pair = KH * 16
     return pl.pallas_call(
         transform_kernel,
         out_shape=jax.ShapeDtypeStruct((A, X, ROWS, L), BF),
-        in_specs=[whole()] * 9,
+        in_specs=[whole()] * 7,
         out_specs=whole(),
         scratch_shapes=[
-            pltpu.VMEM((2 * pair, SEG), F32),
-            pltpu.VMEM((pair, 2 * SEG), BF),
-            pltpu.VMEM((pair, 2 * SEG), F32),
-            pltpu.VMEM((pair, 2 * SEG), BF),
-            pltpu.VMEM((2 * A * 16, SEG), BF),
+            pltpu.VMEM((2, 2, 2 * KH * 8, SEG), F32),
+            pltpu.VMEM((2, KH * 16, 2 * SEG), BF),
+            pltpu.VMEM((2, KH * 16, 2 * SEG), F32),
+            pltpu.VMEM((2, KH * 16, 2 * SEG), BF),
+            pltpu.VMEM((2, KH * 16, 2 * SEG), F32),
+            pltpu.VMEM((2, 2, 2 * A * 8, SEG), BF),
+            pltpu.VMEM((2 * KH * 8, SEG), F32),
+            pltpu.VMEM((KH * 8, 2 * SEG), BF),
             pltpu.VMEM((KH * 8, 2 * SEG), F32),
             pltpu.VMEM((KH * 8, 2 * SEG), F32),
         ],
-        compiler_params=pltpu.CompilerParams(vmem_limit_bytes=48 * MIB),
+        compiler_params=pltpu.CompilerParams(vmem_limit_bytes=36 * MIB),
         name="transform",
     )(
-        fields, t["fwd_pair"], t["fwd_one"], t["inv_pair"], t["inv_one"],
-        t["fwd_rows"], t["inv_rows"], t["cos_twist"], t["sin_twist"],
+        fields, t["forward"], t["backward"], t["fwd_rows"], t["inv_rows"],
+        t["cos_twist"], t["sin_twist"],
     )
 
 

time: 116 us -> 104 us (0.90)
  local copies, waits for them, and re-layouts: 7.61 us -> 0.08 us
  Pallas kernels: 23.4 us -> 20.5 us
    unnamed x40 -> x24, local copies, waits for them, and re-layouts: 7.61 us -> 0.08 us
    pallas_call x1, Pallas kernels: 17 us -> 10.2 us  [transform(): pl.pallas_call(transform_kernel, out_shape=jax.ShapeDtypeStruct((A, X, RO...]
    pallas_call x1, Pallas kernels: 2.39 us -> 6.14 us  [pack(): pl.pallas_call(pack_kernel, out_shape=jax.ShapeDtypeStruct((DEV, ROWS, L)...]
where the time goes in v2:
time: 104 us
  blocking collectives  82.4 us (79%)
  Pallas kernels  20.5 us (20%)
    all_to_all x1, blocking collectives, body(): lax.all_to_all(sent, ('ctx', 'ch'), split_axis=0, concat_axis=0, tiled=True)  45.2 us
    all_to_all x1, blocking collectives, body(): lax.all_to_all(results.reshape(DEV, ROWS, L), ('ctx', 'ch'), split_axis=0...  37.2 us
    pallas_call x1, Pallas kernels, transform(): pl.pallas_call(transform_kernel, out_shape=jax.ShapeDtypeStruct((A, X, RO...  10.2 us
    pallas_call x1, Pallas kernels, pack(): pl.pallas_call(pack_kernel, out_shape=jax.ShapeDtypeStruct((DEV, ROWS, L)...  6.14 us
    pallas_call x1, Pallas kernels, finish(): pl.pallas_call(finish_kernel, out_shape=(jax.ShapeDtypeStruct((SEG, 1024)...  4.1 us

profile of v2, /device:TPU:1, one launch (start us, length us, event | category | flops | bytes accessed | tf_op | source)
XLA Modules:
  0.0 103.7 jit_solution(6213206904278388182)
XLA Ops:
  0.6 6.1 %pack.1 = bf16[128,72,128]{2,1,0:T(8,128)(2,1)} custom-call(s32[1]{0:T(128)} %bitcast.index_ref, bf16[512,1024]{1,0:T(8,128)(2,1)} %q_ref.1, bf16[512,1024]{1,0:T(8,128)(2,1)} %k_ref.1, bf16[512,1024]{1,0:T(8,128)(2,1)} %v_ref.1, bf16[512,1024]{1,0:T(8,128)(2,1)} %o_ref.1, f32[512,1024]{1,0:T(8,128)} %f_hbm.1, ...), custom_call_target="tpu_custom_call" | custom-call | tf_op jit(solution)/shard_map/pack/pallas_call | solution.py:147
  6.8 0.0 copy-start.5
  6.8 0.0 copy-start.6
  6.8 0.0 copy-start.7
  6.8 0.0 copy-start.8
  6.8 0.0 copy-start.9
  6.8 0.0 copy-start.10
  6.9 45.2 %all_to_all.10 = bf16[128,72,128]{2,1,0:T(8,128)(2,1)S(1)} all-to-all(bf16[128,72,128]{2,1,0:T(8,128)(2,1)} %pack.1), channel_id=1, replica_groups=mesh['ctx'=32,'ch'=4] {'ctx','ch'}, dimensions={0} | all-to-all | bytes 4718592 | tf_op jit(solution)/shard_map/all_to_all | solution.py:469
  52.0 0.0 copy-done.5
  52.0 0.0 copy-done.6
  52.0 0.0 copy-done.7
  52.0 0.0 copy-done.8
  52.0 0.0 copy-done.9
  52.0 0.0 copy-done.10
  52.1 0.0 copy-start.11
  52.1 10.2 %transform.1 = bf16[32,4,72,128]{3,2,1,0:T(8,128)(2,1)S(1)} custom-call(bf16[32,4,72,128]{3,2,1,0:T(8,128)(2,1)S(1)} %bitcast.4, bf16[528,256]{1,0:T(8,128)(2,1)S(1)} %copy-done.7, bf16[256,512]{1,0:T(8,128)(2,1)S(1)} %copy-done.8, bf16[4,256,256]{2,1,0:T(8,128)(2,1)S(1)} %copy-done.6, bf16[4,256,256]{2,1,0:T(8,128)(2,1)S(1)} %copy-done.5, ...), custom_call_target="tpu_custom_call" | custom-call | tf_op jit(solution)/shard_map/transform/pallas_call | solution.py:376
  62.3 0.0 copy-start
  62.3 0.0 copy-start.1
  62.3 0.0 copy-start.2
  62.3 0.0 copy-start.3
  62.4 0.0 copy-start.4
  62.4 37.2 %all_to_all.11.in_ref = bf16[128,72,128]{2,1,0:T(8,128)(2,1)S(1)} all-to-all(bf16[128,72,128]{2,1,0:T(8,128)(2,1)S(1)} %bitcast.5), channel_id=1, replica_groups=mesh['ctx'=32,'ch'=4] {'ctx','ch'}, dimensions={0} | all-to-all | bytes 4718592 | tf_op jit(solution)/shard_map/all_to_all | solution.py:471
  99.6 0.0 copy-done.1
  99.6 4.1 %finish.1 = (bf16[512,1024]{1,0:T(8,128)(2,1)}, bf16[512,1024]{1,0:T(8,128)(2,1)}, bf16[512,1024]{1,0:T(8,128)(2,1)}, f32[512,256]{1,0:T(8,128)}) custom-call(bf16[128,72,128]{2,1,0:T(8,128)(2,1)S(1)} %all_to_all.11.in_ref, bf16[512,1024]{1,0:T(8,128)(2,1)S(1)} %copy-done, bf16[512,1024]{1,0:T(8,128)(2,1)S(1)} %copy-done.1, bf16[512,1024]{1,0:T(8,128)(2,1)S(1)} %copy-done.2, ...), custom_call_target="tpu_custom_call" | custom-call | tf_op jit(solution)/shard_map/finish/pallas_call | solution.py:444
  (5 shorter events, 0.0 us)
Async XLA Ops:
  6.8 45.2 %copy-start.5 = (bf16[4,256,256]{2,1,0:T(8,128)(2,1)S(1)}, bf16[4,256,256]{2,1,0:T(8,128)(2,1)}, u32[]{:S(2)}) copy-start(bf16[4,256,256]{2,1,0:T(8,128)(2,1)} %constant.21.clone.ir_ref) | copy-start | bytes 1572868
  6.8 45.2 %copy-start.6 = (bf16[4,256,256]{2,1,0:T(8,128)(2,1)S(1)}, bf16[4,256,256]{2,1,0:T(8,128)(2,1)}, u32[]{:S(2)}) copy-start(bf16[4,256,256]{2,1,0:T(8,128)(2,1)} %constant.20.clone.fr_ref) | copy-start | bytes 1572868
  6.8 45.2 %copy-start.7 = (bf16[528,256]{1,0:T(8,128)(2,1)S(1)}, bf16[528,256]{1,0:T(8,128)(2,1)}, u32[]{:S(2)}) copy-start(bf16[528,256]{1,0:T(8,128)(2,1)} %constant.18.clone.fwd_ref) | copy-start | bytes 811012
  6.8 45.2 %copy-start.8 = (bf16[256,512]{1,0:T(8,128)(2,1)S(1)}, bf16[256,512]{1,0:T(8,128)(2,1)}, u32[]{:S(2)}) copy-start(bf16[256,512]{1,0:T(8,128)(2,1)} %constant.19.clone.inv_ref) | copy-start | bytes 786436
  6.8 45.2 %copy-start.9 = (f32[33,512]{1,0:T(8,128)S(1)}, f32[33,512]{1,0:T(8,128)}, u32[]{:S(2)}) copy-start(f32[33,512]{1,0:T(8,128)} %constant.23.clone.sin_ref) | copy-start | bytes 202756
  6.8 45.2 %copy-start.10 = (f32[33,512]{1,0:T(8,128)S(1)}, f32[33,512]{1,0:T(8,128)}, u32[]{:S(2)}) copy-start(f32[33,512]{1,0:T(8,128)} %constant.22.clone.cos_ref) | copy-start | bytes 202756
  52.1 47.5 %copy-start.11 = (f32[1024]{0:T(1024)S(1)}, f32[1024]{0:T(1024)}, u32[]{:S(2)}) copy-start(f32[1024]{0:T(1024)} %param.18) | copy-start | bytes 12292
  62.3 37.3 %copy-start = (bf16[512,1024]{1,0:T(8,128)(2,1)S(1)}, bf16[512,1024]{1,0:T(8,128)(2,1)}, u32[]{:S(2)}) copy-start(bf16[512,1024]{1,0:T(8,128)(2,1)} %q_ref.1) | copy-start | bytes 3145732
  62.3 37.3 %copy-start.1 = (bf16[512,1024]{1,0:T(8,128)(2,1)S(1)}, bf16[512,1024]{1,0:T(8,128)(2,1)}, u32[]{:S(2)}) copy-start(bf16[512,1024]{1,0:T(8,128)(2,1)} %k_ref.1) | copy-start | bytes 3145732
  62.3 37.3 %copy-start.2 = (bf16[512,1024]{1,0:T(8,128)(2,1)S(1)}, bf16[512,1024]{1,0:T(8,128)(2,1)}, u32[]{:S(2)}) copy-start(bf16[512,1024]{1,0:T(8,128)(2,1)} %v_ref.1) | copy-start | bytes 3145732
  62.3 37.3 %copy-start.3 = (bf16[512,1024]{1,0:T(8,128)(2,1)S(1)}, bf16[512,1024]{1,0:T(8,128)(2,1)}, u32[]{:S(2)}) copy-start(bf16[512,1024]{1,0:T(8,128)(2,1)} %o_ref.1) | copy-start | bytes 3145732
  62.4 37.3 %copy-start.4 = (bf16[512,512]{1,0:T(8,128)(2,1)S(1)}, bf16[512,512]{1,0:T(8,128)(2,1)}, u32[]{:S(2)}) copy-start(bf16[512,512]{1,0:T(8,128)(2,1)} %constant.24.clone.order_hbm.order_ref) | copy-start | bytes 1572868

commit v3 on v2

--- a/solution.py
+++ b/solution.py
@@ -82,35 +82,27 @@
 
 
 def pack_kernel(
-    index_ref, q_hbm, k_hbm, v_hbm, o_hbm, f_hbm, order_hbm, out_ref,
-    fields_ref, taps_ref, order_ref, field_sems, other_sems,
+    q_hbm, k_hbm, v_hbm, o_hbm, f_hbm, out_hbm,
+    fields_ref, taps_ref, order_ref, pair_ref, tail_ref, field_sems, taps_sem, out_sems,
 ):
-    step = pl.program_id(0)
     sources = (k_hbm, v_hbm, q_hbm, o_hbm)
 
     def field_copy(i, n):
-        rows = pl.ds(pl.multiple_of(n * L, L), L)
+        rows = pl.ds(n * L, L)
         return pltpu.make_async_copy(
             sources[i].at[rows], fields_ref.at[i, rows], field_sems.at[n, i]
         )
 
-    def taps_copy():
-        rows = pl.ds(pl.multiple_of(index_ref[0] * L, L), L)
-        return pltpu.make_async_copy(f_hbm.at[rows], taps_ref, other_sems.at[0])
-
-    def order_copy():
-        return pltpu.make_async_copy(order_hbm, order_ref, other_sems.at[1])
-
-    @pl.when(step == 0)
-    def _():
+    rows = pl.ds(pl.multiple_of(lax.axis_index("ch") * L, L), L)
+    taps_copy = pltpu.make_async_copy(f_hbm.at[rows], taps_ref, taps_sem)
+    for n in range(4):
         for i in range(4):
-            field_copy(i, 0).start()
-        order_copy().start()
-        for n in range(1, 4):
-            for i in range(4):
-                field_copy(i, n).start()
-        taps_copy().start()
-        order_copy().wait()
+            field_copy(i, n).start()
+    taps_copy.start()
+    row = lax.broadcasted_iota(jnp.int32, (512, 512), 0)
+    column = lax.broadcasted_iota(jnp.int32, (512, 512), 1)
+    source = row // 2 % 4 * 128 + row // 8 * 2 + row % 2
+    order_ref[...] = jnp.where(column == source, 1.0, 0.0).astype(BF)
 
     def by_owner(field, half):
         columns = jnp.concatenate(
@@ -120,49 +112,56 @@
             order_ref[...], columns, (((1,), (1,)), ((), ())), preferred_element_type=F32
         )
 
-    @pl.when(step < 4)
-    def _():
+    copies = []
+    for n in range(4):
         for i in range(4):
-            field_copy(i, step).wait()
-        rows = pl.ds(pl.multiple_of(step * L, L), L)
-        k, v, q, o = (up(fields_ref[i, rows, :]) for i in range(4))
+            field_copy(i, n).wait()
+        k, v, q, o = (up(fields_ref[i, n * L : (n + 1) * L, :]) for i in range(4))
         both = jnp.concatenate([(k * v).astype(BF), (q * o).astype(BF)], axis=0)
         for half in range(2):
             moved = by_owner(both, half)
             pair = jnp.concatenate(
                 [moved[:, :L].reshape(64, 8, L), moved[:, L:].reshape(64, 8, L)], axis=1
             )
-            out_ref[half * 64 : half * 64 + 64, :, :] = pair.astype(BF)
-
-    @pl.when(step == 4)
-    def _():
-        taps_copy().wait()
-        taps = taps_ref[...].astype(BF)
-        for half in range(2):
-            moved = by_owner(taps, half).reshape(64, 8, L)
-            out_ref[half * 64 : half * 64 + 64, :8, :] = moved.astype(BF)
-
-
-def pack(index, q_in, k_in, v_in, out_grad, filters, order):
+            pair_ref[n, half * 64 : half * 64 + 64, :, :] = pair.astype(BF)
+        copies.append(
+            pltpu.make_async_copy(
+                pair_ref.at[n], out_hbm.at[:, pl.ds(n * 16, 16), :], out_sems.at[n]
+            )
+        )
+        copies[-1].start()
+    taps_copy.wait()
+    taps = taps_ref[...].astype(BF)
+    for half in range(2):
+        moved = by_owner(taps, half).reshape(64, 8, L)
+        tail_ref[half * 64 : half * 64 + 64, :, :] = moved.astype(BF)
+    copies.append(
+        pltpu.make_async_copy(tail_ref, out_hbm.at[:, pl.ds(64, 8), :], out_sems.at[4])
+    )
+    copies[-1].start()
+    for copy in copies:
+        copy.wait()
+
+
+def pack(q_in, k_in, v_in, out_grad, filters):
     return pl.pallas_call(
         pack_kernel,
         out_shape=jax.ShapeDtypeStruct((DEV, ROWS, L), BF),
-        grid_spec=pltpu.PrefetchScalarGridSpec(
-            num_scalar_prefetch=1,
-            grid=(5,),
-            in_specs=[pl.BlockSpec(memory_space=pl.ANY)] * 6,
-            out_specs=pl.BlockSpec((DEV, 16, L), lambda i, s: (0, i, 0)),
-            scratch_shapes=[
-                pltpu.VMEM((4, SEG, 1024), BF),
-                pltpu.VMEM((L, 1024), F32),
-                pltpu.VMEM((512, 512), BF),
-                pltpu.SemaphoreType.DMA((4, 4)),
-                pltpu.SemaphoreType.DMA((2,)),
-            ],
-        ),
+        in_specs=[pl.BlockSpec(memory_space=pl.ANY)] * 5,
+        out_specs=pl.BlockSpec(memory_space=pl.ANY),
+        scratch_shapes=[
+            pltpu.VMEM((4, SEG, 1024), BF),
+            pltpu.VMEM((L, 1024), F32),
+            pltpu.VMEM((512, 512), BF),
+            pltpu.VMEM((4, DEV, 16, L), BF),
+            pltpu.VMEM((DEV, 8, L), BF),
+            pltpu.SemaphoreType.DMA((4, 4)),
+            pltpu.SemaphoreType.DMA,
+            pltpu.SemaphoreType.DMA((5,)),
+        ],
         compiler_params=pltpu.CompilerParams(vmem_limit_bytes=60 * MIB),
         name="pack",
-    )(index, q_in, k_in, v_in, out_grad, filters, order)
+    )(q_in, k_in, v_in, out_grad, filters)
 
 
 def quarters(value):
@@ -399,48 +398,57 @@
 
 
 def finish_kernel(
-    in_ref, q_ref, k_ref, v_ref, o_ref, skip_ref, order_ref, dq_ref, dk_ref, dv_ref, df_ref
+    in_ref, q_ref, k_ref, v_ref, o_ref, skip_ref, order_ref,
+    dq_hbm, dk_hbm, dv_hbm, df_hbm,
+    dq_ref, dk_ref, dv_ref, df_ref, field_sems, taps_sem,
 ):
-    step = pl.program_id(0)
-
     def in_place(rows):
         return lax.dot_general(
             rows.astype(BF), order_ref[...], (((0,), (0,)), ((), ())), preferred_element_type=F32
         )
 
-    for half in range(2):
-        part = up(
-            in_ref[half * 64 : half * 64 + 64, pl.ds(pl.multiple_of(step * 16, 16), 16), :]
-        )
-        rows = jnp.concatenate(
-            [part[:, :8].reshape(512, L), part[:, 8:].reshape(512, L)], axis=1
-        )
-        conv = in_place(rows)
-        for g in range(4):
-            cols = slice(g * 256 + half * 128, g * 256 + half * 128 + 128)
-            state = conv[:L, g * L : (g + 1) * L]
-            back = conv[L:, g * L : (g + 1) * L]
-            q, k, v, o = (up(ref[:, cols]) for ref in (q_ref, k_ref, v_ref, o_ref))
-            skip = skip_ref[:, cols]
-            mixed = state + skip * up((k * v).astype(BF))
-            total = back + skip * up((q * o).astype(BF))
-            dq_ref[:, cols] = (o * mixed).astype(BF)
-            dk_ref[:, cols] = (total * v).astype(BF)
-            dv_ref[:, cols] = (total * k).astype(BF)
-
-    @pl.when(step == 0)
-    def _():
+    copies = []
+    for n in range(4):
+        here = slice(n * L, (n + 1) * L)
         for half in range(2):
-            rows = up(in_ref[half * 64 : half * 64 + 64, 64:72, :]).reshape(512, L)
-            taps = in_place(rows)
-            for n in range(4):
-                df_ref[n * L : (n + 1) * L, half * 128 : half * 128 + 128] = taps[
-                    :, n * L : (n + 1) * L
-                ]
+            part = up(in_ref[half * 64 : half * 64 + 64, n * 16 : n * 16 + 16, :])
+            rows = jnp.concatenate(
+                [part[:, :8].reshape(512, L), part[:, 8:].reshape(512, L)], axis=1
+            )
+            conv = in_place(rows)
+            for g in range(4):
+                cols = slice(g * 256 + half * 128, g * 256 + half * 128 + 128)
+                state = conv[:L, g * L : (g + 1) * L]
+                back = conv[L:, g * L : (g + 1) * L]
+                q, k, v, o = (up(ref[here, cols]) for ref in (q_ref, k_ref, v_ref, o_ref))
+                skip = skip_ref[:, cols]
+                mixed = state + skip * up((k * v).astype(BF))
+                total = back + skip * up((q * o).astype(BF))
+                dq_ref[here, cols] = (o * mixed).astype(BF)
+                dk_ref[here, cols] = (total * v).astype(BF)
+                dv_ref[here, cols] = (total * k).astype(BF)
+        if n == 1:
+            for half in range(2):
+                rows = up(in_ref[half * 64 : half * 64 + 64, 64:72, :]).reshape(512, L)
+                taps = in_place(rows)
+                for m in range(4):
+                    df_ref[m * L : (m + 1) * L, half * 128 : half * 128 + 128] = taps[
+                        :, m * L : (m + 1) * L
+                    ]
+            copies.append(pltpu.make_async_copy(df_ref, df_hbm, taps_sem))
+            copies[-1].start()
+        pairs = ((dq_ref, dq_hbm), (dk_ref, dk_hbm), (dv_ref, dv_hbm))
+        for i, (source, target) in enumerate(pairs):
+            rows = pl.ds(n * L, L)
+            copies.append(
+                pltpu.make_async_copy(source.at[rows], target.at[rows], field_sems.at[n, i])
+            )
+            copies[-1].start()
+    for copy in copies:
+        copy.wait()
 
 
 def finish(fields, q_in, k_in, v_in, out_grad, skip, order):
-    field = pl.BlockSpec((L, 1024), lambda i: (i, 0))
     return pl.pallas_call(
         finish_kernel,
         out_shape=(
@@ -449,23 +457,24 @@
             jax.ShapeDtypeStruct((SEG, 1024), BF),
             jax.ShapeDtypeStruct((SEG, 256), F32),
         ),
-        grid=(4,),
-        in_specs=[pl.BlockSpec((DEV, ROWS, L), lambda i: (0, 0, 0))]
-        + [field] * 4
-        + [
-            pl.BlockSpec((1, 1024), lambda i: (0, 0)),
-            pl.BlockSpec((512, 512), lambda i: (0, 0)),
+        in_specs=[whole()] * 7,
+        out_specs=(pl.BlockSpec(memory_space=pl.ANY),) * 4,
+        scratch_shapes=[
+            pltpu.VMEM((SEG, 1024), BF),
+            pltpu.VMEM((SEG, 1024), BF),
+            pltpu.VMEM((SEG, 1024), BF),
+            pltpu.VMEM((SEG, 256), F32),
+            pltpu.SemaphoreType.DMA((4, 3)),
+            pltpu.SemaphoreType.DMA,
         ],
-        out_specs=(field, field, field, pl.BlockSpec((SEG, 256), lambda i: (0, 0))),
-        compiler_params=pltpu.CompilerParams(vmem_limit_bytes=40 * MIB),
+        compiler_params=pltpu.CompilerParams(vmem_limit_bytes=24 * MIB),
         name="finish",
     )(fields, q_in, k_in, v_in, out_grad, skip, order)
 
 
 def body(q_in, k_in, v_in, out_grad, filters, skip):
     t = {name: jnp.asarray(value) for name, value in constants().items()}
-    index = lax.axis_index("ch").astype(jnp.int32).reshape(1)
-    sent = pack(index, q_in, k_in, v_in, out_grad, filters, t["order"])
+    sent = pack(q_in, k_in, v_in, out_grad, filters)
     columns = lax.all_to_all(sent, ("ctx", "ch"), split_axis=0, concat_axis=0, tiled=True)
     results = transform(columns.reshape(A, X, ROWS, L), t)
     blocks = lax.all_to_all(

time: 104 us -> 102 us (0.981)
  Pallas kernels: 20.5 us -> 17.9 us
    pallas_call x1, Pallas kernels: 6.14 us -> 4.5 us  [pack(): pl.pallas_call(pack_kernel, out_shape=jax.ShapeDtypeStruct((DEV, ROWS, L)...]
    pallas_call x1, Pallas kernels: 4.1 us -> 2.99 us  [finish(): pl.pallas_call(finish_kernel, out_shape=(jax.ShapeDtypeStruct((SEG, 1024)...]
where the time goes in v3:
time: 102 us; the launch traced here: 101 us
  blocking collectives  82.4 us (81%)
  Pallas kernels  17.9 us (18%)
    all_to_all x1, blocking collectives, body(): lax.all_to_all(sent, ('ctx', 'ch'), split_axis=0, concat_axis=0, tiled=True)  45.2 us
    all_to_all x1, blocking collectives, body(): lax.all_to_all(results.reshape(DEV, ROWS, L), ('ctx', 'ch'), split_axis=0...  37.2 us
    pallas_call x1, Pallas kernels, transform(): pl.pallas_call(transform_kernel, out_shape=jax.ShapeDtypeStruct((A, X, RO...  10.4 us
    pallas_call x1, Pallas kernels, pack(): pl.pallas_call(pack_kernel, out_shape=jax.ShapeDtypeStruct((DEV, ROWS, L)...  4.5 us
    pallas_call x1, Pallas kernels, finish(): pl.pallas_call(finish_kernel, out_shape=(jax.ShapeDtypeStruct((SEG, 1024)...  2.99 us

profile of v3, /device:TPU:1, one launch (start us, length us, event | category | flops | bytes accessed | tf_op | source)
XLA Modules:
  0.0 101.3 jit_solution(15180376416307384092)
XLA Ops:
  0.6 4.5 %pack.1 = bf16[128,72,128]{2,1,0:T(8,128)(2,1)} custom-call(bf16[512,1024]{1,0:T(8,128)(2,1)} %q_ref.1, bf16[512,1024]{1,0:T(8,128)(2,1)} %k_ref.1, bf16[512,1024]{1,0:T(8,128)(2,1)} %v_ref.1, bf16[512,1024]{1,0:T(8,128)(2,1)} %o_ref.1, f32[512,1024]{1,0:T(8,128)} %f_hbm.1), custom_call_target="tpu_custom_call" | custom-call | tf_op jit(solution)/shard_map/pack/pallas_call | solution.py:147
  5.1 0.0 copy-start.5
  5.1 0.0 copy-start.6
  5.2 0.0 copy-start.7
  5.2 0.0 copy-start.8
  5.2 0.0 copy-start.9
  5.2 0.0 copy-start.10
  5.2 45.2 %all_to_all.10 = bf16[128,72,128]{2,1,0:T(8,128)(2,1)S(1)} all-to-all(bf16[128,72,128]{2,1,0:T(8,128)(2,1)} %pack.1), channel_id=1, replica_groups=mesh['ctx'=32,'ch'=4] {'ctx','ch'}, dimensions={0} | all-to-all | bytes 4718592 | tf_op jit(solution)/shard_map/all_to_all | solution.py:478
  50.4 0.0 copy-done.5
  50.4 0.0 copy-done.6
  50.4 0.0 copy-done.7
  50.4 0.0 copy-done.8
  50.4 0.0 copy-done.9
  50.4 0.0 copy-done.10
  50.4 0.0 copy-start.11
  50.4 10.4 %transform.1 = bf16[32,4,72,128]{3,2,1,0:T(8,128)(2,1)S(1)} custom-call(bf16[32,4,72,128]{3,2,1,0:T(8,128)(2,1)S(1)} %bitcast.3, bf16[528,256]{1,0:T(8,128)(2,1)S(1)} %copy-done.7, bf16[256,512]{1,0:T(8,128)(2,1)S(1)} %copy-done.8, bf16[4,256,256]{2,1,0:T(8,128)(2,1)S(1)} %copy-done.6, bf16[4,256,256]{2,1,0:T(8,128)(2,1)S(1)} %copy-done.5, ...), custom_call_target="tpu_custom_call" | custom-call | tf_op jit(solution)/shard_map/transform/pallas_call | solution.py:375
  60.9 0.0 copy-start
  60.9 0.0 copy-start.1
  60.9 0.0 copy-start.2
  60.9 0.0 copy-start.3
  60.9 0.0 copy-start.4
  60.9 37.2 %all_to_all.11.in_ref = bf16[128,72,128]{2,1,0:T(8,128)(2,1)S(1)} all-to-all(bf16[128,72,128]{2,1,0:T(8,128)(2,1)S(1)} %bitcast.4), channel_id=1, replica_groups=mesh['ctx'=32,'ch'=4] {'ctx','ch'}, dimensions={0} | all-to-all | bytes 4718592 | tf_op jit(solution)/shard_map/all_to_all | solution.py:480
  98.2 0.0 copy-done.11
  98.2 3.0 %finish.1 = (bf16[512,1024]{1,0:T(8,128)(2,1)}, bf16[512,1024]{1,0:T(8,128)(2,1)}, bf16[512,1024]{1,0:T(8,128)(2,1)}, f32[512,256]{1,0:T(8,128)}) custom-call(bf16[128,72,128]{2,1,0:T(8,128)(2,1)S(1)} %all_to_all.11.in_ref, bf16[512,1024]{1,0:T(8,128)(2,1)S(1)} %copy-done, bf16[512,1024]{1,0:T(8,128)(2,1)S(1)} %copy-done.1, bf16[512,1024]{1,0:T(8,128)(2,1)S(1)} %copy-done.2, ...), custom_call_target="tpu_custom_call" | custom-call | tf_op jit(solution)/shard_map/finish/pallas_call | solution.py:452
  (5 shorter events, 0.0 us)
Async XLA Ops:
  5.1 45.2 %copy-start.5 = (bf16[4,256,256]{2,1,0:T(8,128)(2,1)S(1)}, bf16[4,256,256]{2,1,0:T(8,128)(2,1)}, u32[]{:S(2)}) copy-start(bf16[4,256,256]{2,1,0:T(8,128)(2,1)} %constant.17.clone.ir_ref) | copy-start | bytes 1572868
  5.1 45.2 %copy-start.6 = (bf16[4,256,256]{2,1,0:T(8,128)(2,1)S(1)}, bf16[4,256,256]{2,1,0:T(8,128)(2,1)}, u32[]{:S(2)}) copy-start(bf16[4,256,256]{2,1,0:T(8,128)(2,1)} %constant.16.clone.fr_ref) | copy-start | bytes 1572868
  5.2 45.2 %copy-start.7 = (bf16[528,256]{1,0:T(8,128)(2,1)S(1)}, bf16[528,256]{1,0:T(8,128)(2,1)}, u32[]{:S(2)}) copy-start(bf16[528,256]{1,0:T(8,128)(2,1)} %constant.14.clone.fwd_ref) | copy-start | bytes 811012
  5.2 45.2 %copy-start.8 = (bf16[256,512]{1,0:T(8,128)(2,1)S(1)}, bf16[256,512]{1,0:T(8,128)(2,1)}, u32[]{:S(2)}) copy-start(bf16[256,512]{1,0:T(8,128)(2,1)} %constant.15.clone.inv_ref) | copy-start | bytes 786436
  5.2 45.2 %copy-start.9 = (f32[33,512]{1,0:T(8,128)S(1)}, f32[33,512]{1,0:T(8,128)}, u32[]{:S(2)}) copy-start(f32[33,512]{1,0:T(8,128)} %constant.19.clone.sin_ref) | copy-start | bytes 202756
  5.2 45.2 %copy-start.10 = (f32[33,512]{1,0:T(8,128)S(1)}, f32[33,512]{1,0:T(8,128)}, u32[]{:S(2)}) copy-start(f32[33,512]{1,0:T(8,128)} %constant.18.clone.cos_ref) | copy-start | bytes 202756
  50.4 47.8 %copy-start.11 = (f32[1024]{0:T(1024)S(1)}, f32[1024]{0:T(1024)}, u32[]{:S(2)}) copy-start(f32[1024]{0:T(1024)} %param.18) | copy-start | bytes 12292
  60.9 37.3 %copy-start = (bf16[512,1024]{1,0:T(8,128)(2,1)S(1)}, bf16[512,1024]{1,0:T(8,128)(2,1)}, u32[]{:S(2)}) copy-start(bf16[512,1024]{1,0:T(8,128)(2,1)} %q_ref.1) | copy-start | bytes 3145732
  60.9 37.3 %copy-start.1 = (bf16[512,1024]{1,0:T(8,128)(2,1)S(1)}, bf16[512,1024]{1,0:T(8,128)(2,1)}, u32[]{:S(2)}) copy-start(bf16[512,1024]{1,0:T(8,128)(2,1)} %k_ref.1) | copy-start | bytes 3145732
  60.9 37.3 %copy-start.2 = (bf16[512,1024]{1,0:T(8,128)(2,1)S(1)}, bf16[512,1024]{1,0:T(8,128)(2,1)}, u32[]{:S(2)}) copy-start(bf16[512,1024]{1,0:T(8,128)(2,1)} %v_ref.1) | copy-start | bytes 3145732
  60.9 37.3 %copy-start.3 = (bf16[512,1024]{1,0:T(8,128)(2,1)S(1)}, bf16[512,1024]{1,0:T(8,128)(2,1)}, u32[]{:S(2)}) copy-start(bf16[512,1024]{1,0:T(8,128)(2,1)} %o_ref.1) | copy-start | bytes 3145732
  60.9 37.3 %copy-start.4 = (bf16[512,512]{1,0:T(8,128)(2,1)S(1)}, bf16[512,512]{1,0:T(8,128)(2,1)}, u32[]{:S(2)}) copy-start(bf16[512,512]{1,0:T(8,128)(2,1)} %constant.20.clone.order_ref) | copy-start | bytes 1572868

commit v4 on v3

--- a/solution.py
+++ b/solution.py
@@ -41,7 +41,7 @@
     sin_block = low(np.sin(angle)).astype(np.float64)
     cos_block[np.abs(cos_block) < 1e-6] = 0.0
     sin_block[np.abs(sin_block) < 1e-6] = 0.0
-    forward = np.concatenate([cos_block, -sin_block], 0)
+    forward = np.stack([cos_block, -sin_block], 1).reshape(2 * KH, A)
     weight = np.where((k == 0) | (k == A), 1.0, 2.0) / PERIOD
     backward = np.concatenate([weight * cos_block, -(weight * sin_block)[1:A]], 0).T
     l = np.arange(L)[:, None]
@@ -182,8 +182,8 @@
     s = sin_ref[k : k + 1, :]
     found = []
     for sums_ref in fields:
-        re = sums_ref[k * 8 : k * 8 + 8, :]
-        im = sums_ref[(KH + k) * 8 : (KH + k) * 8 + 8, :]
+        both = up(sums_ref[k * 16 : k * 16 + 16, :])
+        re, im = both[:8], both[8:]
         parts = butterfly(quarters(re * c + im * s), quarters(im * c - re * s), -1)
         found.append(jnp.concatenate([part for pair in parts for part in pair], axis=1))
     return found
@@ -193,9 +193,9 @@
     ref[row : row + 8 * len(pieces), :] = jnp.concatenate(pieces, axis=0).astype(BF)
 
 
-def twist_back(rows_ref, cos_ref, sin_ref, row, k):
-    re = [rows_ref[row : row + 8, n * 256 : n * 256 + L] for n in range(4)]
-    im = [rows_ref[row : row + 8, n * 256 + L : n * 256 + 256] for n in range(4)]
+def twist_back(rows_ref, cos_ref, sin_ref, rows, k):
+    re = [up(rows_ref[rows, n * 256 : n * 256 + L]) for n in range(4)]
+    im = [up(rows_ref[rows, n * 256 + L : n * 256 + 256]) for n in range(4)]
     real, imag = [], []
     for n, (ur, ui) in enumerate(butterfly(re, im, 1)):
         c = cos_ref[k : k + 1, n * L : (n + 1) * L]
@@ -249,7 +249,7 @@
     def row_sums(data, table, out):
         def piece(n):
             cols = slice(n * 256, (n + 1) * 256)
-            out[:, cols] = mm(data[:, cols], table[n])
+            out[:, cols] = mm(data[:, cols], table[n]).astype(out.dtype)
 
         return [lambda n=n: piece(n) for n in range(4)]
 
@@ -282,14 +282,19 @@
 
         return [lambda k=k: piece(k) for k in range(KH)]
 
-    def back_twist(rows, place, out):
+    def back_twist(rows, height, outs):
         def piece(ks):
-            parts = [twist_back(rows, cos_ref, sin_ref, place(k), k) for k in ks]
-            store_rows(out, ks[0] * 8, [parts[0][0], parts[1][0]])
-            if len(ks) == 3:
-                store_rows(out, A * 8, [parts[2][0], parts[1][1]])
-            else:
-                store_rows(out, (A + ks[0]) * 8, [parts[0][1], parts[1][1]])
+            parts = [
+                twist_back(rows, cos_ref, sin_ref, slice(k * height, (k + 1) * height), k)
+                for k in ks
+            ]
+            for i, out in enumerate(outs):
+                own = [(re[i * 8 : i * 8 + 8], im[i * 8 : i * 8 + 8]) for re, im in parts]
+                store_rows(out, ks[0] * 8, [own[0][0], own[1][0]])
+                if len(ks) == 3:
+                    store_rows(out, A * 8, [own[2][0], own[1][1]])
+                else:
+                    store_rows(out, (A + ks[0]) * 8, [own[0][1], own[1][1]])
 
         return [lambda ks=ks: piece(ks) for ks in PAIRS]
 
@@ -312,12 +317,7 @@
         return row_sums(y_ref.at[g % 2], ir_ref, v_ref.at[g % 2])
 
     def back_twists(g):
-        pieces = []
-        for f in range(2):
-            pieces += back_twist(
-                v_ref.at[g % 2], lambda k, f=f: k * 16 + f * 8, u_ref.at[g % 2, f]
-            )
-        return pieces
+        return back_twist(v_ref.at[g % 2], 16, [u_ref.at[g % 2, f] for f in range(2)])
 
     def filter_sums():
         def piece(half):
@@ -358,7 +358,7 @@
         if g + 2 < X:
             interleave(block_sums(g + 2), [])
     interleave(row_sums(filt_z, ir_ref, filt_ref), back_twists(X - 1))
-    interleave(results(X - 1), back_twist(filt_ref, lambda k: k * 8, u_ref.at[0, 0]))
+    interleave(results(X - 1), back_twist(filt_ref, 8, [u_ref.at[0, 0]]))
 
     result = mm(inv_ref[...], u_ref[0, 0]) * (1.0 / 256.0)
     place = lax.broadcasted_iota(jnp.int32, (A * 8, L), 0) % 8 // 2

time: 102 us -> 100 us (0.980)
  Pallas kernels: 17.9 us -> 16.7 us
    pallas_call x1, Pallas kernels: 10.4 us -> 9.16 us  [transform(): pl.pallas_call(transform_kernel, out_shape=jax.ShapeDtypeStruct((A, X, RO...]
where the time goes in v4:
time: 100 us
  blocking collectives  82.6 us (83%)
  Pallas kernels  16.7 us (17%)
    all_to_all x1, blocking collectives, body(): lax.all_to_all(sent, ('ctx', 'ch'), split_axis=0, concat_axis=0, tiled=True)  45.2 us
    all_to_all x1, blocking collectives, body(): lax.all_to_all(results.reshape(DEV, ROWS, L), ('ctx', 'ch'), split_axis=0...  37.4 us
    pallas_call x1, Pallas kernels, transform(): pl.pallas_call(transform_kernel, out_shape=jax.ShapeDtypeStruct((A, X, RO...  9.16 us
    pallas_call x1, Pallas kernels, pack(): pl.pallas_call(pack_kernel, out_shape=jax.ShapeDtypeStruct((DEV, ROWS, L)...  4.5 us
    pallas_call x1, Pallas kernels, finish(): pl.pallas_call(finish_kernel, out_shape=(jax.ShapeDtypeStruct((SEG, 1024)...  3 us

profile of v4, /device:TPU:1, one launch (start us, length us, event | category | flops | bytes accessed | tf_op | source)
XLA Modules:
  0.0 100.3 jit_solution(8427059668407567314)
XLA Ops:
  0.6 4.5 %pack.1 = bf16[128,72,128]{2,1,0:T(8,128)(2,1)} custom-call(bf16[512,1024]{1,0:T(8,128)(2,1)} %q_ref.1, bf16[512,1024]{1,0:T(8,128)(2,1)} %k_ref.1, bf16[512,1024]{1,0:T(8,128)(2,1)} %v_ref.1, bf16[512,1024]{1,0:T(8,128)(2,1)} %o_ref.1, f32[512,1024]{1,0:T(8,128)} %f_hbm.1), custom_call_target="tpu_custom_call" | custom-call | tf_op jit(solution)/shard_map/pack/pallas_call | solution.py:147
  5.1 0.0 copy-start.5
  5.1 0.0 copy-start.6
  5.2 0.0 copy-start.7
  5.2 0.0 copy-start.8
  5.2 0.0 copy-start.9
  5.2 0.0 copy-start.10
  5.2 45.2 %all_to_all.10 = bf16[128,72,128]{2,1,0:T(8,128)(2,1)S(1)} all-to-all(bf16[128,72,128]{2,1,0:T(8,128)(2,1)} %pack.1), channel_id=1, replica_groups=mesh['ctx'=32,'ch'=4] {'ctx','ch'}, dimensions={0} | all-to-all | bytes 4718592 | tf_op jit(solution)/shard_map/all_to_all | solution.py:478
  50.4 0.0 copy-done.5
  50.4 0.0 copy-done.6
  50.4 0.0 copy-done.7
  50.4 0.0 copy-done.8
  50.4 0.0 copy-done.9
  50.4 0.0 copy-done.10
  50.4 0.0 copy-start.11
  50.4 9.2 %transform.1 = bf16[32,4,72,128]{3,2,1,0:T(8,128)(2,1)S(1)} custom-call(bf16[32,4,72,128]{3,2,1,0:T(8,128)(2,1)S(1)} %bitcast.3, bf16[528,256]{1,0:T(8,128)(2,1)S(1)} %copy-done.7, bf16[256,512]{1,0:T(8,128)(2,1)S(1)} %copy-done.8, bf16[4,256,256]{2,1,0:T(8,128)(2,1)S(1)} %copy-done.6, bf16[4,256,256]{2,1,0:T(8,128)(2,1)S(1)} %copy-done.5, ...), custom_call_target="tpu_custom_call" | custom-call | tf_op jit(solution)/shard_map/transform/pallas_call | solution.py:375
  59.6 0.0 copy-start
  59.6 0.0 copy-start.1
  59.6 0.0 copy-start.2
  59.6 0.0 copy-start.3
  59.6 0.0 copy-start.4
  59.7 37.4 %all_to_all.11.in_ref = bf16[128,72,128]{2,1,0:T(8,128)(2,1)S(1)} all-to-all(bf16[128,72,128]{2,1,0:T(8,128)(2,1)S(1)} %bitcast.4), channel_id=1, replica_groups=mesh['ctx'=32,'ch'=4] {'ctx','ch'}, dimensions={0} | all-to-all | bytes 4718592 | tf_op jit(solution)/shard_map/all_to_all | solution.py:480
  97.1 0.0 copy-done.1
  97.1 3.0 %finish.1 = (bf16[512,1024]{1,0:T(8,128)(2,1)}, bf16[512,1024]{1,0:T(8,128)(2,1)}, bf16[512,1024]{1,0:T(8,128)(2,1)}, f32[512,256]{1,0:T(8,128)}) custom-call(bf16[128,72,128]{2,1,0:T(8,128)(2,1)S(1)} %all_to_all.11.in_ref, bf16[512,1024]{1,0:T(8,128)(2,1)S(1)} %copy-done, bf16[512,1024]{1,0:T(8,128)(2,1)S(1)} %copy-done.1, bf16[512,1024]{1,0:T(8,128)(2,1)S(1)} %copy-done.2, ...), custom_call_target="tpu_custom_call" | custom-call | tf_op jit(solution)/shard_map/finish/pallas_call | solution.py:452
  (5 shorter events, 0.0 us)
Async XLA Ops:
  5.1 45.2 %copy-start.5 = (bf16[4,256,256]{2,1,0:T(8,128)(2,1)S(1)}, bf16[4,256,256]{2,1,0:T(8,128)(2,1)}, u32[]{:S(2)}) copy-start(bf16[4,256,256]{2,1,0:T(8,128)(2,1)} %constant.17.clone.ir_ref) | copy-start | bytes 1572868
  5.1 45.2 %copy-start.6 = (bf16[4,256,256]{2,1,0:T(8,128)(2,1)S(1)}, bf16[4,256,256]{2,1,0:T(8,128)(2,1)}, u32[]{:S(2)}) copy-start(bf16[4,256,256]{2,1,0:T(8,128)(2,1)} %constant.16.clone.fr_ref) | copy-start | bytes 1572868
  5.2 45.2 %copy-start.7 = (bf16[528,256]{1,0:T(8,128)(2,1)S(1)}, bf16[528,256]{1,0:T(8,128)(2,1)}, u32[]{:S(2)}) copy-start(bf16[528,256]{1,0:T(8,128)(2,1)} %constant.14.clone.fwd_ref) | copy-start | bytes 811012
  5.2 45.2 %copy-start.8 = (bf16[256,512]{1,0:T(8,128)(2,1)S(1)}, bf16[256,512]{1,0:T(8,128)(2,1)}, u32[]{:S(2)}) copy-start(bf16[256,512]{1,0:T(8,128)(2,1)} %constant.15.clone.inv_ref) | copy-start | bytes 786436
  5.2 45.2 %copy-start.9 = (f32[33,512]{1,0:T(8,128)S(1)}, f32[33,512]{1,0:T(8,128)}, u32[]{:S(2)}) copy-start(f32[33,512]{1,0:T(8,128)} %constant.19.clone.sin_ref) | copy-start | bytes 202756
  5.2 45.2 %copy-start.10 = (f32[33,512]{1,0:T(8,128)S(1)}, f32[33,512]{1,0:T(8,128)}, u32[]{:S(2)}) copy-start(f32[33,512]{1,0:T(8,128)} %constant.18.clone.cos_ref) | copy-start | bytes 202756
  50.4 46.7 %copy-start.11 = (f32[1024]{0:T(1024)S(1)}, f32[1024]{0:T(1024)}, u32[]{:S(2)}) copy-start(f32[1024]{0:T(1024)} %param.18) | copy-start | bytes 12292
  59.6 37.5 %copy-start = (bf16[512,1024]{1,0:T(8,128)(2,1)S(1)}, bf16[512,1024]{1,0:T(8,128)(2,1)}, u32[]{:S(2)}) copy-start(bf16[512,1024]{1,0:T(8,128)(2,1)} %q_ref.1) | copy-start | bytes 3145732
  59.6 37.5 %copy-start.1 = (bf16[512,1024]{1,0:T(8,128)(2,1)S(1)}, bf16[512,1024]{1,0:T(8,128)(2,1)}, u32[]{:S(2)}) copy-start(bf16[512,1024]{1,0:T(8,128)(2,1)} %k_ref.1) | copy-start | bytes 3145732
  59.6 37.5 %copy-start.2 = (bf16[512,1024]{1,0:T(8,128)(2,1)S(1)}, bf16[512,1024]{1,0:T(8,128)(2,1)}, u32[]{:S(2)}) copy-start(bf16[512,1024]{1,0:T(8,128)(2,1)} %v_ref.1) | copy-start | bytes 3145732
  59.6 37.5 %copy-start.3 = (bf16[512,1024]{1,0:T(8,128)(2,1)S(1)}, bf16[512,1024]{1,0:T(8,128)(2,1)}, u32[]{:S(2)}) copy-start(bf16[512,1024]{1,0:T(8,128)(2,1)} %o_ref.1) | copy-start | bytes 3145732
  59.6 37.5 %copy-start.4 = (bf16[512,512]{1,0:T(8,128)(2,1)S(1)}, bf16[512,512]{1,0:T(8,128)(2,1)}, u32[]{:S(2)}) copy-start(bf16[512,512]{1,0:T(8,128)(2,1)} %constant.20.clone.order_ref) | copy-start | bytes 1572868

commit v5 on v4

--- a/solution.py
+++ b/solution.py
@@ -88,14 +88,14 @@
     sources = (k_hbm, v_hbm, q_hbm, o_hbm)
 
     def field_copy(i, n):
-        rows = pl.ds(n * L, L)
+        rows = pl.ds(n * L, 2 * L if n == 2 else L)
         return pltpu.make_async_copy(
             sources[i].at[rows], fields_ref.at[i, rows], field_sems.at[n, i]
         )
 
     rows = pl.ds(pl.multiple_of(lax.axis_index("ch") * L, L), L)
     taps_copy = pltpu.make_async_copy(f_hbm.at[rows], taps_ref, taps_sem)
-    for n in range(4):
+    for n in range(3):
         for i in range(4):
             field_copy(i, n).start()
     taps_copy.start()
@@ -114,7 +114,7 @@
 
     copies = []
     for n in range(4):
-        for i in range(4):
+        for i in range(4 if n < 3 else 0):
             field_copy(i, n).wait()
         k, v, q, o = (up(fields_ref[i, n * L : (n + 1) * L, :]) for i in range(4))
         both = jnp.concatenate([(k * v).astype(BF), (q * o).astype(BF)], axis=0)
@@ -155,7 +155,7 @@
             pltpu.VMEM((512, 512), BF),
             pltpu.VMEM((4, DEV, 16, L), BF),
             pltpu.VMEM((DEV, 8, L), BF),
-            pltpu.SemaphoreType.DMA((4, 4)),
+            pltpu.SemaphoreType.DMA((3, 4)),
             pltpu.SemaphoreType.DMA,
             pltpu.SemaphoreType.DMA((5,)),
         ],
@@ -438,8 +438,8 @@
             copies.append(pltpu.make_async_copy(df_ref, df_hbm, taps_sem))
             copies[-1].start()
         pairs = ((dq_ref, dq_hbm), (dk_ref, dk_hbm), (dv_ref, dv_hbm))
-        for i, (source, target) in enumerate(pairs):
-            rows = pl.ds(n * L, L)
+        for i, (source, target) in enumerate(pairs if n > 0 else ()):
+            rows = pl.ds(0, 2 * L) if n == 1 else pl.ds(n * L, L)
             copies.append(
                 pltpu.make_async_copy(source.at[rows], target.at[rows], field_sems.at[n, i])
             )

time: 100 us -> 99.8 us (level)
  no operation moved by 1% of the time
where the time goes in v5:
time: 99.8 us; the launch traced here: 99.7 us
  blocking collectives  82.4 us (83%)
  Pallas kernels  16.4 us (16%)
    all_to_all x1, blocking collectives, body(): lax.all_to_all(sent, ('ctx', 'ch'), split_axis=0, concat_axis=0, tiled=True)  45.2 us
    all_to_all x1, blocking collectives, body(): lax.all_to_all(results.reshape(DEV, ROWS, L), ('ctx', 'ch'), split_axis=0...  37.2 us
    pallas_call x1, Pallas kernels, transform(): pl.pallas_call(transform_kernel, out_shape=jax.ShapeDtypeStruct((A, X, RO...  9.16 us
    pallas_call x1, Pallas kernels, pack(): pl.pallas_call(pack_kernel, out_shape=jax.ShapeDtypeStruct((DEV, ROWS, L)...  4.25 us
    pallas_call x1, Pallas kernels, finish(): pl.pallas_call(finish_kernel, out_shape=(jax.ShapeDtypeStruct((SEG, 1024)...  3 us

profile of v5, /device:TPU:1, one launch (start us, length us, event | category | flops | bytes accessed | tf_op | source)
XLA Modules:
  0.0 99.7 jit_solution(14931743989519733340)
XLA Ops:
  0.6 4.2 %pack.1 = bf16[128,72,128]{2,1,0:T(8,128)(2,1)} custom-call(bf16[512,1024]{1,0:T(8,128)(2,1)} %q_ref.1, bf16[512,1024]{1,0:T(8,128)(2,1)} %k_ref.1, bf16[512,1024]{1,0:T(8,128)(2,1)} %v_ref.1, bf16[512,1024]{1,0:T(8,128)(2,1)} %o_ref.1, f32[512,1024]{1,0:T(8,128)} %f_hbm.1), custom_call_target="tpu_custom_call" | custom-call | tf_op jit(solution)/shard_map/pack/pallas_call | solution.py:147
  4.9 0.0 copy-start.5
  4.9 0.0 copy-start.6
  4.9 0.0 copy-start.7
  4.9 0.0 copy-start.8
  4.9 0.0 copy-start.9
  4.9 0.0 copy-start.10
  5.0 45.2 %all_to_all.10 = bf16[128,72,128]{2,1,0:T(8,128)(2,1)S(1)} all-to-all(bf16[128,72,128]{2,1,0:T(8,128)(2,1)} %pack.1), channel_id=1, replica_groups=mesh['ctx'=32,'ch'=4] {'ctx','ch'}, dimensions={0} | all-to-all | bytes 4718592 | tf_op jit(solution)/shard_map/all_to_all | solution.py:478
  50.1 0.0 copy-done.5
  50.1 0.0 copy-done.6
  50.1 0.0 copy-done.7
  50.2 0.0 copy-start.11
  50.2 9.2 %transform.1 = bf16[32,4,72,128]{3,2,1,0:T(8,128)(2,1)S(1)} custom-call(bf16[32,4,72,128]{3,2,1,0:T(8,128)(2,1)S(1)} %bitcast.3, bf16[528,256]{1,0:T(8,128)(2,1)S(1)} %copy-done.7, bf16[256,512]{1,0:T(8,128)(2,1)S(1)} %copy-done.8, bf16[4,256,256]{2,1,0:T(8,128)(2,1)S(1)} %copy-done.6, bf16[4,256,256]{2,1,0:T(8,128)(2,1)S(1)} %copy-done.5, ...), custom_call_target="tpu_custom_call" | custom-call | tf_op jit(solution)/shard_map/transform/pallas_call | solution.py:375
  59.3 0.0 copy-start
  59.3 0.0 copy-start.1
  59.4 0.0 copy-start.2
  59.4 0.0 copy-start.3
  59.4 0.0 copy-start.4
  59.4 37.2 %all_to_all.11.in_ref = bf16[128,72,128]{2,1,0:T(8,128)(2,1)S(1)} all-to-all(bf16[128,72,128]{2,1,0:T(8,128)(2,1)S(1)} %bitcast.4), channel_id=1, replica_groups=mesh['ctx'=32,'ch'=4] {'ctx','ch'}, dimensions={0} | all-to-all | bytes 4718592 | tf_op jit(solution)/shard_map/all_to_all | solution.py:480
  96.6 0.0 copy-done.1
  96.6 0.0 copy-done.2
  96.6 0.0 copy-done.3
  96.7 0.0 copy-done.4
  96.7 3.0 %finish.1 = (bf16[512,1024]{1,0:T(8,128)(2,1)}, bf16[512,1024]{1,0:T(8,128)(2,1)}, bf16[512,1024]{1,0:T(8,128)(2,1)}, f32[512,256]{1,0:T(8,128)}) custom-call(bf16[128,72,128]{2,1,0:T(8,128)(2,1)S(1)} %all_to_all.11.in_ref, bf16[512,1024]{1,0:T(8,128)(2,1)S(1)} %copy-done, bf16[512,1024]{1,0:T(8,128)(2,1)S(1)} %copy-done.1, bf16[512,1024]{1,0:T(8,128)(2,1)S(1)} %copy-done.2, ...), custom_call_target="tpu_custom_call" | custom-call | tf_op jit(solution)/shard_map/finish/pallas_call | solution.py:452
  (5 shorter events, 0.0 us)
Async XLA Ops:
  4.9 45.2 %copy-start.5 = (bf16[4,256,256]{2,1,0:T(8,128)(2,1)S(1)}, bf16[4,256,256]{2,1,0:T(8,128)(2,1)}, u32[]{:S(2)}) copy-start(bf16[4,256,256]{2,1,0:T(8,128)(2,1)} %constant.17.clone.ir_ref) | copy-start | bytes 1572868
  4.9 45.2 %copy-start.6 = (bf16[4,256,256]{2,1,0:T(8,128)(2,1)S(1)}, bf16[4,256,256]{2,1,0:T(8,128)(2,1)}, u32[]{:S(2)}) copy-start(bf16[4,256,256]{2,1,0:T(8,128)(2,1)} %constant.16.clone.fr_ref) | copy-start | bytes 1572868
  4.9 45.2 %copy-start.7 = (bf16[528,256]{1,0:T(8,128)(2,1)S(1)}, bf16[528,256]{1,0:T(8,128)(2,1)}, u32[]{:S(2)}) copy-start(bf16[528,256]{1,0:T(8,128)(2,1)} %constant.14.clone.fwd_ref) | copy-start | bytes 811012
  4.9 45.2 %copy-start.8 = (bf16[256,512]{1,0:T(8,128)(2,1)S(1)}, bf16[256,512]{1,0:T(8,128)(2,1)}, u32[]{:S(2)}) copy-start(bf16[256,512]{1,0:T(8,128)(2,1)} %constant.15.clone.inv_ref) | copy-start | bytes 786436
  4.9 45.2 %copy-start.9 = (f32[33,512]{1,0:T(8,128)S(1)}, f32[33,512]{1,0:T(8,128)}, u32[]{:S(2)}) copy-start(f32[33,512]{1,0:T(8,128)} %constant.19.clone.sin_ref) | copy-start | bytes 202756
  4.9 45.2 %copy-start.10 = (f32[33,512]{1,0:T(8,128)S(1)}, f32[33,512]{1,0:T(8,128)}, u32[]{:S(2)}) copy-start(f32[33,512]{1,0:T(8,128)} %constant.18.clone.cos_ref) | copy-start | bytes 202756
  50.2 46.5 %copy-start.11 = (f32[1024]{0:T(1024)S(1)}, f32[1024]{0:T(1024)}, u32[]{:S(2)}) copy-start(f32[1024]{0:T(1024)} %param.18) | copy-start | bytes 12292
  59.3 37.3 %copy-start = (bf16[512,1024]{1,0:T(8,128)(2,1)S(1)}, bf16[512,1024]{1,0:T(8,128)(2,1)}, u32[]{:S(2)}) copy-start(bf16[512,1024]{1,0:T(8,128)(2,1)} %q_ref.1) | copy-start | bytes 3145732
  59.3 37.3 %copy-start.1 = (bf16[512,1024]{1,0:T(8,128)(2,1)S(1)}, bf16[512,1024]{1,0:T(8,128)(2,1)}, u32[]{:S(2)}) copy-start(bf16[512,1024]{1,0:T(8,128)(2,1)} %k_ref.1) | copy-start | bytes 3145732
  59.4 37.3 %copy-start.2 = (bf16[512,1024]{1,0:T(8,128)(2,1)S(1)}, bf16[512,1024]{1,0:T(8,128)(2,1)}, u32[]{:S(2)}) copy-start(bf16[512,1024]{1,0:T(8,128)(2,1)} %v_ref.1) | copy-start | bytes 3145732
  59.4 37.3 %copy-start.3 = (bf16[512,1024]{1,0:T(8,128)(2,1)S(1)}, bf16[512,1024]{1,0:T(8,128)(2,1)}, u32[]{:S(2)}) copy-start(bf16[512,1024]{1,0:T(8,128)(2,1)} %o_ref.1) | copy-start | bytes 3145732
  59.4 37.3 %copy-start.4 = (bf16[512,512]{1,0:T(8,128)(2,1)S(1)}, bf16[512,512]{1,0:T(8,128)(2,1)}, u32[]{:S(2)}) copy-start(bf16[512,512]{1,0:T(8,128)(2,1)} %constant.20.clone.order_ref) | copy-start | bytes 1572868
